TPU v7x, 128 devices: a whole 4x4x4 slice. The times are simulated.
128 devices in a mesh: member: 2 (over z_lo), grid: 64 (over y, x, z_hi, core).
Axes of the slice: x: 4, y: 4, z: 4 (z_hi: 2, z_lo: 2; z = z_hi * 2 + z_lo), core: 2. Of those that a mesh axis runs over, the one named last changes fastest.
Arguments:
- latent: bfloat16 [8, 8192, 1024], P('member', 'grid'), may hold values from -6 to 6
- grid_in: bfloat16 [8, 8192, 1024], P('member', 'grid'), may hold values from -6 to 6
- w_src: bfloat16 [1024, 1024], replicated, may hold values from -0.1875 to 0.1875
- w_tgt: bfloat16 [1024, 1024], replicated, may hold values from -0.1875 to 0.1875
- w_mix: bfloat16 [1024, 1024], replicated, may hold values from -0.1875 to 0.1875
- w_out: bfloat16 [1024, 100], replicated, may hold values from -0.1875 to 0.1875
- truth: float32 [100, 8192], P(None, 'grid'), may hold values from -6 to 6
- area: float32 [8192], P('grid'), may hold values from 0.2 to 30, as said below
- nbr: int32 [16, 8192], P(None, 'grid'), may hold values from 0 to 255
- mask: int32 [16, 8192], P(None, 'grid'), may hold values 0 or 1
Outputs:
- d_latent: bfloat16 [8, 8192, 1024], P('member', 'grid')
- d_grid: bfloat16 [8, 8192, 1024], P('member', 'grid')
- grad_src: float32 [1024, 1024], P('grid')
- grad_tgt: float32 [1024, 1024], P('grid')
- grad_mix: float32 [1024, 1024], P('grid')
- grad_out: float32 [1024, 100], P('grid')
Inputs may be any that keep to these rules, and one draw needn't show every extreme that they name: area weights are positive.
All inputs are finite; a program needn't handle non-finite values. No bound on the sum of `mask` on one device may be relied on, other than what follows from the above.
Results may differ from a plain program's by a relative error of at most 0.039.
Values may be sent and summed in bfloat16 or wider, within the bound.
A program may use at most 128 MiB of HBM per device.

v0:
```python
import math

import jax
import jax.numpy as jnp
from jax import lax
from jax.sharding import PartitionSpec as P

HALO = 64


smooth_sq = 0.0025
fair_weight = 0.95
norm_eps = 1e-05


def padded(array, sides, width):
    for axis, dim in sides:
        size, length = (lax.axis_size(axis), array.shape[dim])
        up = [(i, (i + 1) % size) for i in range(size)]
        down = [(j, i) for i, j in up]
        last = lax.slice_in_dim(array, length - width, length, axis=dim)
        leading = lax.slice_in_dim(array, 0, width, axis=dim)
        before = lax.ppermute(last, axis, up)
        after = lax.ppermute(leading, axis, down)
        array = jnp.concatenate([before, array, after], axis=dim)
    return array


def shifted(value, axis, steps):
    count = lax.axis_size(axis)
    pairs = [(source, (source + steps) % count) for source in range(count)]
    return lax.ppermute(value, axis, pairs)


def silu_grad(value):
    sig = jax.nn.sigmoid(value)
    return sig * (1.0 + value * (1.0 - sig))


def layer_stats(hsum):
    centre = hsum - jnp.mean(hsum, axis=-1, keepdims=True)
    var = jnp.mean(centre * centre, axis=-1, keepdims=True)
    inv_std = lax.rsqrt(var + norm_eps)
    return (centre * inv_std, inv_std)


def on_device(latent, grid_in, w_src, w_tgt, w_mix, w_out, truth, area, nbr, mask):
    members_here = latent.shape[0]
    rows = grid_in.shape[1]
    src_rows = latent.shape[1]
    width = latent.shape[2]
    tiles = lax.axis_size("grid")
    extended = padded(latent, (("grid", 1),), HALO)
    proj_ext = jnp.einsum(
        "msd,de->mse", extended, w_src, preferred_element_type=jnp.float32
    ).astype(jnp.bfloat16)
    ext_rows = proj_ext.shape[1]
    columns = jnp.arange(ext_rows, dtype=jnp.int32)
    proj_tgt = jnp.einsum("msd,de->mse", grid_in, w_tgt, preferred_element_type=jnp.float32).astype(
        jnp.bfloat16
    )
    tgt_f = proj_tgt.astype(jnp.float32)
    maskf = mask.astype(jnp.float32)

    def forward_step(acc, slot):
        index, weight = slot
        picker = (index[:, None] == columns[None, :]).astype(jnp.bfloat16)
        pre = (
            jnp.einsum("se,med->msd", picker, proj_ext, preferred_element_type=jnp.float32) + tgt_f
        )
        return (acc + weight[None, :, None] * jax.nn.silu(pre), None)

    acc, _ = lax.scan(
        forward_step, jnp.zeros((members_here, rows, width), jnp.float32), (nbr, maskf)
    )
    agg = (0.25 * acc).astype(jnp.bfloat16)
    hsum = grid_in.astype(jnp.float32) + jnp.einsum(
        "msd,de->mse", agg, w_mix, preferred_element_type=jnp.float32
    )
    nh, inv_std = layer_stats(hsum)
    normed = nh.astype(jnp.bfloat16)
    outputs = jnp.einsum("msd,df->mfs", normed, w_out, preferred_element_type=jnp.float32)
    everyone = lax.all_gather(outputs, "member", axis=0, tiled=True)
    count = everyone.shape[0]
    diff = outputs[:, None] - everyone[None]
    root = jnp.sqrt(diff * diff + smooth_sq)
    pair_grad = jnp.sum(diff / root, axis=1)
    miss = outputs - truth[None]
    skill = jnp.sqrt(miss * miss + smooth_sq)
    dy = (
        area[None, None, :]
        * (miss / skill / count - fair_weight / (count * (count - 1)) * pair_grad)
    ).astype(jnp.bfloat16)
    g_out = jnp.einsum("msd,mfs->df", normed, dy, preferred_element_type=jnp.float32)
    dnorm = jnp.einsum("mfs,df->msd", dy, w_out, preferred_element_type=jnp.float32)
    dh = inv_std * (
        dnorm
        - jnp.mean(dnorm, axis=-1, keepdims=True)
        - nh * jnp.mean(dnorm * nh, axis=-1, keepdims=True)
    )
    dh = dh.astype(jnp.bfloat16)
    g_mix = jnp.einsum("msd,mse->de", agg, dh, preferred_element_type=jnp.float32)
    dagg = (
        jnp.einsum("mse,de->msd", dh, w_mix, preferred_element_type=jnp.float32)
        .astype(jnp.bfloat16)
        .astype(jnp.float32)
    )

    def backward_step(carry, slot):
        dq_acc, dp_acc = carry
        index, weight = slot
        picker = (index[:, None] == columns[None, :]).astype(jnp.bfloat16)
        pre = (
            jnp.einsum("se,med->msd", picker, proj_ext, preferred_element_type=jnp.float32) + tgt_f
        )
        dpre = 0.25 * weight[None, :, None] * dagg * silu_grad(pre)
        spread = jnp.einsum(
            "se,msd->med",
            picker.astype(jnp.float32),
            dpre,
            preferred_element_type=jnp.float32,
            precision=lax.Precision.HIGHEST,
        )
        return ((dq_acc + dpre, dp_acc + spread), None)

    init = (
        jnp.zeros((members_here, rows, width), jnp.float32),
        jnp.zeros((members_here, ext_rows, width), jnp.float32),
    )
    (dq_acc, dp_acc), _ = lax.scan(backward_step, init, (nbr, maskf))
    lower_rim = dp_acc[:, :HALO]
    upper_rim = dp_acc[:, HALO + src_rows :]
    owned = dp_acc[:, HALO : HALO + src_rows]
    from_next = shifted(lower_rim.astype(jnp.bfloat16), "grid", -1).astype(lower_rim.dtype)
    from_prev = shifted(upper_rim.astype(jnp.bfloat16), "grid", 1).astype(upper_rim.dtype)
    owned = owned.at[:, src_rows - HALO :].add(from_next)
    owned = owned.at[:, :HALO].add(from_prev)
    dp = owned.astype(jnp.bfloat16)
    dq = dq_acc.astype(jnp.bfloat16)
    g_tgt = jnp.einsum("msd,mse->de", grid_in, dq, preferred_element_type=jnp.float32)
    g_src = jnp.einsum("msd,mse->de", latent, dp, preferred_element_type=jnp.float32)
    d_grid = (
        dh.astype(jnp.float32)
        + jnp.einsum("mse,de->msd", dq, w_tgt, preferred_element_type=jnp.float32)
    ).astype(jnp.bfloat16)
    d_latent = jnp.einsum("mse,de->msd", dp, w_src, preferred_element_type=jnp.float32).astype(
        jnp.bfloat16
    )
    summed = (
        lax.psum(g_src.astype(jnp.bfloat16), "member").astype(jnp.float32),
        lax.psum(g_tgt.astype(jnp.bfloat16), "member").astype(jnp.float32),
        lax.psum(g_mix.astype(jnp.bfloat16), "member").astype(jnp.float32),
        lax.psum(g_out.astype(jnp.bfloat16), "member").astype(jnp.float32),
    )
    summed = (
        lax.psum_scatter(summed[0], "grid", scatter_dimension=0, tiled=True),
        lax.psum_scatter(summed[1], "grid", scatter_dimension=0, tiled=True),
        lax.psum_scatter(summed[2], "grid", scatter_dimension=0, tiled=True),
        lax.psum_scatter(summed[3], "grid", scatter_dimension=0, tiled=True),
    )
    scale = 1.0 / math.sqrt(rows * tiles * count)
    return (
        d_latent,
        d_grid,
        summed[0] * scale,
        summed[1] * scale,
        summed[2] * scale,
        summed[3] * scale,
    )


def solution(mesh):
    in_specs = (
        P("member", "grid", None),
        P("member", "grid", None),
        P(),
        P(),
        P(),
        P(),
        P(None, "grid"),
        P("grid"),
        P(None, "grid"),
        P(None, "grid"),
    )
    out_specs = (
        P("member", "grid", None),
        P("member", "grid", None),
        P("grid", None),
        P("grid", None),
        P("grid", None),
        P("grid", None),
    )
    return jax.shard_map(
        on_device, mesh=mesh, in_specs=in_specs, out_specs=out_specs, check_vma=False
    )
```

profile of v0, /device:TPU:0, one launch (start us, length us, event | category | flops | bytes accessed | tf_op | source)
XLA Modules:
  0.0 1867.2 jit_solution(11488479464079496646)
XLA Ops:
  8.8 8.1 collective-permute-start.1
  16.9 4.6 fusion.50
  23.9 4.9 fusion.29
  28.8 94.0 %while.26 = (s32[]{:T(128)}, f32[4,128,1024]{2,1,0:T(8,128)}, f32[16,128]{1,0:T(8,128)S(1)}, s32[16,128]{1,0:T(8,128)}, bf16[4,256,1024]{2,1,0:T(8,128)(2,1)}, /...) while((s32[]{:T(128)}, f32[4,128,1024]{2,1,0:T(8,128)}, f32[16,128]{1,0:T(8,128)S(1)}, ...), condition=%wide.region_1.2_spmd.clone, body=%wide.region_0.1_spmd.clone.sunk | while | flops 272662528 | bytes 8391791 | solution.py:73
  29.6 4.6 select_add_fusion.4
  34.8 5.2 select_add_fusion.4
  40.8 5.2 select_add_fusion.4
  46.7 5.2 select_add_fusion.4
  52.6 5.2 select_add_fusion.4
  58.5 5.2 select_add_fusion.4
  64.4 5.2 select_add_fusion.4
  70.3 5.2 select_add_fusion.4
  76.2 5.2 select_add_fusion.4
  82.1 5.2 select_add_fusion.4
  88.0 5.2 select_add_fusion.4
  93.9 5.2 select_add_fusion.4
  99.8 5.2 select_add_fusion.4
  105.7 5.2 select_add_fusion.4
  111.6 5.2 select_add_fusion.4
  117.6 5.2 select_add_fusion.4
  128.1 6.7 all_gather.3
  143.5 175.0 %while.27 = (s32[]{:T(128)}, f32[4,128,1024]{2,1,0:T(8,128)}, f32[4,256,1024]{1,2,0:T(8,128)}, f32[16,128]{1,0:T(8,128)S(1)}, f32[4,128,1024]{2,1,0:T(8,128)}, /...) while((s32[]{:T(128)}, f32[4,128,1024]{2,1,0:T(8,128)}, ...), condition=%wide.region_8.9_spmd.clone, body=%wide.region_7.8_spmd.clone.sunk | while | flops 1887502464 | bytes 56626872 | solution.py:130
  144.2 5.5 select_add_fusion.5
  154.5 6.1 select_add_fusion.5
  165.5 6.1 select_add_fusion.5
  176.5 6.1 select_add_fusion.5
  187.4 6.1 select_add_fusion.5
  198.4 6.1 select_add_fusion.5
  209.4 6.1 select_add_fusion.5
  220.4 6.1 select_add_fusion.5
  231.3 6.1 select_add_fusion.5
  242.3 6.1 select_add_fusion.5
  253.3 6.1 select_add_fusion.5
  264.3 6.1 select_add_fusion.5
  275.2 6.1 select_add_fusion.5
  286.2 6.1 select_add_fusion.5
  297.2 6.1 select_add_fusion.5
  308.1 6.1 select_add_fusion.5
  318.4 5.4 copy.39
  345.2 171.1 %all-reduce.3.cloned.1.call-done = (bf16[1024,1024]{0,1:T(8,128)(2,1)}, bf16[1024,1024]{0,1:T(8,128)(2,1)}, bf16[1024,1024]{1,0:T(8,128)(2,1)}, bf16[1024,100]{1,0:T(8,128)(2,1)}) async-done(((bf16[1024,1024]{0,1:T(8,128)(2,1)}, bf16[1024,1024]{0,1:T(8,128)(2,1)}, bf16[1024,1024]{1,0:T(8,128)(2,1)}, bf16[1024,100]{1,0:T(8,128)(2,1)}), (bf16[1024,1024]{0,1:T(8,128)(2,1)}, bf16[1024,1024]{0,1:T(8,128)(2,1)}, ...) | async-done | bytes 6496272 | tf_op jit(solution)/shard_map/psum | solution.py:150
  518.2 4.1 copy.55
  522.4 4.2 copy.57
  526.7 4.0 convert_element_type.114
  530.7 4.6 add_convert_fusion
  537.6 314.6 %reduce-scatter.11.cloned.1.call-done = f32[16,100]{1,0:T(8,128)} async-done(((f32[1024,100]{1,0:T(8,128)}), f32[16,100]{1,0:T(8,128)}) %reduce-scatter.11.cloned.1.call-update) | async-done | bytes 6416 | tf_op jit(solution)/shard_map/reduce_scatter | solution.py:159
  853.5 334.2 %reduce-scatter.13.cloned.1.call-done = f32[16,1024]{1,0:T(8,128)} async-done(((f32[1024,1024]{1,0:T(8,128)}), f32[16,1024]{1,0:T(8,128)}) %reduce-scatter.13.cloned.1.call-update) | async-done | bytes 65552
  1189.6 333.7 %reduce-scatter.15.cloned.1.call-done = f32[16,1024]{1,0:T(8,128)} async-done(((f32[1024,1024]{1,0:T(8,128)}), f32[16,1024]{1,0:T(8,128)}) %reduce-scatter.15.cloned.1.call-update) | async-done | bytes 65552
  1525.2 333.6 %reduce-scatter.17.cloned.1.call-done = f32[16,1024]{1,0:T(8,128)} async-done(((f32[1024,1024]{1,0:T(8,128)}), f32[16,1024]{1,0:T(8,128)}) %reduce-scatter.17.cloned.1.call-update) | async-done | bytes 65552
  (234 shorter events, 138.5 us)
Async XLA Ops:
  7.2 16.7 copy-start
  7.2 9.7 copy-start.12
  7.2 509.1 %all-reduce.3.cloned.1.call-start = ((), (), s32[]{:S(2)}) async-start(), calls=%async_computation.8 | async-start | bytes 13107200 | tf_op jit(solution)/shard_map/psum | solution.py:150
  8.7 15.2 collective-permute-start
  8.8 15.1 collective-permute-start.1
  16.9 7.0 copy-start.8
  28.8 94.0 %copy-start.15 = (bf16[4,128,1024]{2,1,0:T(8,128)(2,1)S(1)}, bf16[4,128,1024]{2,1,0:T(8,128)(2,1)}, u32[]{:S(2)}) copy-start(bf16[4,128,1024]{2,1,0:T(8,128)(2,1)} %param.19) | copy-start | bytes 3145732
  126.3 10.2 copy-start.3
  127.5 8.1 copy-start.11
  127.5 8.1 copy-start.13
  138.1 2.7 copy-start.14
  144.2 5.5 copy-start.1
  151.9 1.9 copy-start.2
  154.5 6.2 copy-start.1
  162.8 1.9 copy-start.2
  165.5 6.2 copy-start.1
  173.8 1.9 copy-start.2
  176.5 6.2 copy-start.1
  184.8 1.9 copy-start.2
  187.4 6.2 copy-start.1
  198.4 6.2 copy-start.1
  206.7 1.9 copy-start.2
  209.4 6.2 copy-start.1
  220.4 6.2 copy-start.1
  228.7 1.9 copy-start.2
  231.3 6.2 copy-start.1
  242.3 6.2 copy-start.1
  253.3 6.2 copy-start.1
  264.2 6.2 copy-start.1
  275.2 6.2 copy-start.1
  283.5 1.9 copy-start.2
  286.2 6.2 copy-start.1
  297.2 6.2 copy-start.1
  305.5 1.9 copy-start.2
  308.1 6.2 copy-start.1
  326.3 7.6 copy-start.17
  326.4 7.6 copy-start.16
  326.4 14.5 collective-permute-start.3
  330.1 10.5 collective-permute-start.2
  334.0 2.6 copy-start.4
  334.0 6.7 copy-start.5
  336.6 4.0 slice-start
  338.2 4.4 copy-start.9
  345.2 507.1 %reduce-scatter.11.cloned.1.call-start = ((), (), s32[]{:S(2)}) async-start(), calls=%async_computation.4 | async-start | bytes 532480 | tf_op jit(solution)/shard_map/reduce_scatter | solution.py:159
  518.1 669.6 %reduce-scatter.13.cloned.1.call-start = ((), (), s32[]{:S(2)}) async-start(), calls=%async_computation.5 | async-start | bytes 4259840
  522.3 1001.0 %reduce-scatter.15.cloned.1.call-start = ((), (), s32[]{:S(2)}) async-start(), calls=%async_computation.6 | async-start | bytes 4259840
  526.6 1332.1 %reduce-scatter.17.cloned.1.call-start = ((), (), s32[]{:S(2)}) async-start(), calls=%async_computation.7 | async-start | bytes 4259840
  530.7 4.6 copy-start.7
  (11 other events, 19.7 us)
Sparse Core Ops, SparseCore 0:
  345.3 170.9 all-reduce.2
  518.8 333.4 reduce-scatter.10
  854.6 333.0 reduce-scatter.12
  1190.1 333.1 reduce-scatter.14
  1525.5 333.1 reduce-scatter.16
where the time goes:
time: 1870 us
  waiting for transfers between devices  1490 us (80%)
  matrix products  248 us (13%)
  local copies, waits for them, and re-layouts  77.4 us (4%)
    unnamed x8, waiting for transfers between devices  1000 us
    reduce_scatter x1, waiting for transfers between devices, on_device(): lax.psum_scatter(summed[3], 'grid', scatter_dimension=0, tiled=True)  315 us
    psum x1, waiting for transfers between devices, on_device(): lax.psum(g_src.astype(jnp.bfloat16), 'member').astype(jnp.float32)  171 us
    dot_general x16, matrix products, backward_step(): jnp.einsum('se,med->msd', picker, proj_ext, preferred_element_type=jnp.fl...  97.6 us
    dot_general x16, matrix products, forward_step(): jnp.einsum('se,med->msd', picker, proj_ext, preferred_element_type=jnp.fl...  82.7 us
  transfers between devices with their start and end apart: 9, of which 8 were waited for; matrix products, arithmetic and copies ran while one was open for 2% of the time, Pallas kernels for 0%

commit v1 on v0

v1 whole, which is shorter than its diff:
```python
import math

import jax
import jax.numpy as jnp
from jax import lax
from jax.experimental import pallas as pl
from jax.experimental.pallas import tpu as pltpu
from jax.sharding import PartitionSpec as P

HALO = 64
SMOOTH = 0.0025
FAIR = 0.95
EPS = 1e-05
BF = jnp.bfloat16
F32 = jnp.float32
MESH = pl.DeviceIdType.MESH
CW = 256
NY, NX, NZ, NC = 4, 4, 2, 2
FP = 128


def dot(a, b):
    return lax.dot_general(a, b, (((1,), (0,)), ((), ())), preferred_element_type=F32)


def dot_nt(a, b):
    return lax.dot_general(a, b, (((1,), (1,)), ((), ())), preferred_element_type=F32)


def dot_tn(a, b):
    return lax.dot_general(a, b, (((0,), (0,)), ((), ())), preferred_element_type=F32)


class Place:
    def __init__(self):
        self.me = lax.axis_index("member")
        t = lax.axis_index("grid")
        tiles = NY * NX * NZ * NC
        self.y, self.x, self.z, self.c = t // 16, (t // 4) % 4, (t // 2) % 2, t % 2
        self.up = (self.me, (t + 1) % tiles)
        self.down = (self.me, (t + tiles - 1) % tiles)
        self.mate = (1 - self.me, t)
        self.core = self.at(c=1 - self.c)
        self.y_ring = (self.at(y=(self.y + 1) % 4), self.at(y=(self.y + 3) % 4))
        self.x_ring = (self.at(x=(self.x + 1) % 4), self.at(x=(self.x + 3) % 4))
        self.z_far = (self.me, self.at(z=1 - self.z)[1])
        self.z_both = (1 - self.me, self.z_far[1])
        self.partners = (self.up, self.down, self.core, *self.y_ring, *self.x_ring,
                         self.mate, self.z_far, self.z_both)

    def at(self, y=None, x=None, z=None, c=None):
        y = self.y if y is None else y
        x = self.x if x is None else x
        z = self.z if z is None else z
        c = self.c if c is None else c
        return (self.me, y * 16 + x * 4 + z * 2 + c)


class Wire:
    def __init__(self, send, recv):
        self.send, self.recv, self.used = send, recv, 0

    def copy(self, src, dst, device):
        at = self.used
        self.used += 1
        return pltpu.make_async_remote_copy(
            src_ref=src, dst_ref=dst, send_sem=self.send.at[at], recv_sem=self.recv.at[at],
            device_id=device, device_id_type=MESH)


def add_into(dst, *others):
    total = dst[...].astype(F32)
    for o in others:
        total = total + o[...].astype(F32)
    dst[...] = total.astype(BF)


class Ring:
    def __init__(self, wire, p, ring, block, a, b, d):
        self.wire, self.p, self.ring, self.block = wire, p, ring, block
        self.a, self.b, self.d = a, b, d
        self.nxt, self.prv = (p + 1) % 4, (p + 3) % 4

    def start(self):
        w, (plus, minus), block = self.wire, self.ring, self.block
        opp = (self.p + 2) % 4
        self.first = [w.copy(block(opp, 0), self.a.at[0], plus),
                      w.copy(block(opp, 1), self.a.at[1], minus)]
        self.second = [w.copy(block(self.nxt, 1), self.b.at[0], plus),
                       w.copy(block(self.prv, 0), self.b.at[1], minus)]
        for one in self.first + self.second:
            one.start()

    def middle(self):
        w, (plus, minus), block = self.wire, self.ring, self.block
        self.third = [w.copy(block(self.nxt, 0), self.d.at[0], plus),
                      w.copy(block(self.prv, 1), self.d.at[1], minus)]
        self.first[0].wait()
        add_into(block(self.nxt, 0), self.a.at[0])
        self.third[0].start()
        self.first[1].wait()
        add_into(block(self.prv, 1), self.a.at[1])
        self.third[1].start()

    def finish(self):
        for one in self.second + self.third:
            one.wait()
        add_into(self.block(self.p, 0), self.b.at[1], self.d.at[0])
        add_into(self.block(self.p, 1), self.b.at[0], self.d.at[1])


class Half:
    def __init__(self, place, wire, part, held, cols, y_first, bufs, zbuf):
        self.place, self.wire, self.zbuf, self.cols = place, wire, zbuf, cols
        self.part, self.held = part, held
        y, x = place.y, place.x

        def wide_y(d, h):
            return held.at[d, pl.ds(2 * h, 2), :, :, cols]

        def wide_x(d, h):
            return held.at[pl.ds(2 * h, 2), d, :, :, cols]

        def thin_x(d, h):
            return held.at[y, d, h, :, cols]

        def thin_y(d, h):
            return held.at[d, x, h, :, cols]

        on_y, on_x = (y, place.y_ring), (x, place.x_ring)
        if y_first:
            self.one = Ring(wire, *on_y, wide_y, *bufs[:3])
            self.two = Ring(wire, *on_x, thin_x, *bufs[3:])
        else:
            self.one = Ring(wire, *on_x, wide_x, *bufs[:3])
            self.two = Ring(wire, *on_y, thin_y, *bufs[3:])

    def start(self):
        cols = self.cols
        self.cross = [self.wire.copy(self.part.at[1 - self.place.c, yy, :, :, :, cols],
                                     self.held.at[yy, :, :, :, cols], self.place.core) for yy in range(NY)]
        for one in self.cross:
            one.start()

    def s1(self):
        for one in self.cross:
            one.wait()
        cols = self.cols

        def add(yy, _):
            add_into(self.held.at[yy, :, :, :, cols], self.part.at[self.place.c, yy, :, :, :, cols])
            return 0

        lax.fori_loop(0, NY, add, 0)
        self.one.start()

    def s2(self):
        self.one.middle()

    def s3(self):
        self.one.finish()
        self.two.start()

    def s4(self):
        self.two.middle()

    def s5(self):
        self.two.finish()
        p = self.place
        mine = self.held.at[p.y, p.x]
        self.last = [self.wire.copy(mine.at[p.z, :, self.cols], self.zbuf.at[0], p.mate),
                     self.wire.copy(mine.at[1 - p.z, :, self.cols], self.zbuf.at[1], p.z_far),
                     self.wire.copy(mine.at[1 - p.z, :, self.cols], self.zbuf.at[2], p.z_both)]
        for one in self.last:
            one.start()

    def s6(self, scale):
        p = self.place
        for one in self.last:
            one.wait()
        total = self.held[p.y, p.x, p.z, :, self.cols].astype(F32)
        for k in range(3):
            total = total + self.zbuf[k].astype(F32)
        return total * scale


def put(part, block, cols):
    for b in range(NY * NX * NZ * NC):
        part[b % 2, b // 16, (b // 4) % 4, (b // 2) % 2, :, cols] = block[b * 16:(b + 1) * 16]


def body(scale, lat, grid, wsrc_in, wtgt_in, wmix_in, wout_in, truth_in, area_in, nbr, mask,
         d_latent, d_grid, o_src, o_tgt, o_mix, o_out,
         wsrc, wtgt, wmix, wout, truth, area,
         pick, pick_t, hits, hits_t, maskb, proj, tgt, slope, slope_sum, agg, normed, inv, ys, dys, dh, dq, dpe,
         agg_x, normed_x, grid_x, lat_x,
         halo, rims, part_src, part_tgt, part_mix, held_src, held_tgt, held_mix, *rest):
    send_sem, recv_sem, halo_send, halo_recv, rim_send, rim_recv, y_send, y_recv, load_sem = rest[-9:]
    bufs = rest[:-9]
    members, rows, width = grid.shape
    nbrs = nbr.shape[0]
    fields = wout_in.shape[0]
    ext = rows + 2 * HALO
    tiles = width // CW
    flat = members * rows
    place = Place()
    wire = Wire(send_sem, recv_sem)

    barrier = pltpu.get_barrier_semaphore()
    for partner in place.partners:
        pl.semaphore_signal(barrier, inc=1, device_id=partner, device_id_type=MESH)
    loads = [pltpu.make_async_copy(src, dst, load_sem.at[i])
             for i, (src, dst) in enumerate(((wtgt_in, wtgt), (wsrc_in, wsrc), (wmix_in, wmix)))]
    for one in loads:
        one.start()

    def copies(src_up, src_down, dst, sems, m):
        return (
            pltpu.make_async_remote_copy(
                src_ref=src_up, dst_ref=dst.at[m, pl.ds(0, HALO)],
                send_sem=sems[0].at[0, m], recv_sem=sems[1].at[0, m],
                device_id=place.up, device_id_type=MESH),
            pltpu.make_async_remote_copy(
                src_ref=src_down, dst_ref=dst.at[m, pl.ds(HALO, HALO)],
                send_sem=sems[0].at[1, m], recv_sem=sems[1].at[1, m],
                device_id=place.down, device_id_type=MESH),
        )

    def halo_copies(m):
        return copies(lat.at[m, pl.ds(rows - HALO, HALO)], lat.at[m, pl.ds(0, HALO)], halo,
                      (halo_send, halo_recv), m)

    def rim_copies(m):
        return copies(dpe.at[m, pl.ds(HALO + rows, HALO)], dpe.at[m, pl.ds(0, HALO)], rims,
                      (rim_send, rim_recv), m)

    def y_copy(m):
        return pltpu.make_async_remote_copy(
            src_ref=ys.at[m], dst_ref=ys.at[members + m],
            send_sem=y_send.at[m], recv_sem=y_recv.at[m],
            device_id=place.mate, device_id_type=MESH)

    pl.semaphore_wait(barrier, len(place.partners))
    for m in range(members):
        for one in halo_copies(m):
            one.start()

    truth[...] = jnp.zeros_like(truth)
    truth[0:fields, :] = truth_in[...]
    truth[...] = truth[...].T
    area[...] = jnp.broadcast_to(area_in[...], (rows, FP)).T
    wout[...] = jnp.zeros_like(wout)
    wout[0:fields, :] = wout_in[...]

    code = jnp.where(mask[...] != 0, nbr[...], -1).astype(F32)
    code_t = jnp.concatenate([code, jnp.zeros((rows - nbrs, rows), F32)], axis=0).T
    lane = lax.broadcasted_iota(jnp.int32, (rows, ext), 1).astype(F32)
    sub = lax.broadcasted_iota(jnp.int32, (ext, rows), 0).astype(F32)
    count = jnp.zeros((rows, 1), F32)
    for k in range(nbrs):
        col = code_t[:, k:k + 1]
        on = jnp.where(col >= 0.0, 1.0, 0.0)
        one = (col == lane).astype(F32).astype(BF)
        one_t = (code[k:k + 1, :] == sub).astype(F32).astype(BF)
        pick[k] = one
        maskb[k] = jnp.broadcast_to(on, (rows, 128)).astype(BF)
        count = count + on
        pick_t[:, k * rows:(k + 1) * rows] = one_t
        if k == 0:
            hits[...] = one
            hits_t[...] = one_t
        else:
            hits[...] += one
            hits_t[...] += one_t

    def columns(step, first=0, last=tiles):
        def inner(c, _):
            step(pl.ds(pl.multiple_of(c * CW, CW), CW))
            return 0

        lax.fori_loop(first, last, inner, 0)

    def own_tgt(cols):
        got = (0.5 * dot(grid[...].reshape(flat, width), wtgt[:, cols]).astype(BF)).astype(BF)
        tgt[:, :, cols] = got.reshape(members, rows, CW)

    def own_src(cols):
        got = (0.5 * dot(lat[...].reshape(flat, width), wsrc[:, cols]).astype(BF)).astype(BF)
        proj[:, HALO:HALO + rows, cols] = got.reshape(members, rows, CW)

    loads[0].wait()
    columns(own_tgt)
    loads[1].wait()
    columns(own_src)

    def turn_grid(m, _):
        grid_x[:, pl.ds(pl.multiple_of(m * rows, rows), rows)] = grid[m].T
        return 0

    lax.fori_loop(0, members, turn_grid, 0)
    loads[2].wait()

    gb = 16

    def forward(m, _):
        for one in halo_copies(m):
            one.wait()
        edge = (0.5 * dot(halo[m], wsrc[...]).astype(BF)).astype(BF)
        proj[m, 0:HALO] = edge[0:HALO]
        proj[m, HALO + rows:ext] = edge[HALO:2 * HALO]

        def column(cols):
            table = proj[m, :, cols]
            linear = dot(hits[...], table) + count * tgt[m, :, cols].astype(F32)
            for at in range(0, rows, gb):
                got = dot(pick[:, at:at + gb, :].reshape(nbrs * gb, ext), table).astype(BF)
                got = got.reshape(nbrs, gb, CW)
                base = tgt[m, at:at + gb, cols]
                acc = None
                acc_s = None
                for k in range(nbrs):
                    on = maskb[k, at:at + gb, :]
                    u = got[k] + jnp.concatenate([on] * (CW // 128), axis=1) * base
                    t = jnp.tanh(u)
                    p = u * t
                    s = (t + u) - t * p
                    acc = p if k == 0 else acc + p
                    acc_s = s if k == 0 else acc_s + s
                    slope[m, k, at:at + gb, cols] = s
                agg[m, at:at + gb, cols] = (0.25 * (linear[at:at + gb] + acc.astype(F32))).astype(BF)
                slope_sum[m, at:at + gb, cols] = (acc_s.astype(F32) + count[at:at + gb]).astype(BF)

        columns(column)
        h = grid[m].astype(F32) + dot(agg[m], wmix[...])
        mean = jnp.sum(h, axis=1, keepdims=True) * (1.0 / width)
        centre = h - mean
        var = jnp.sum(centre * centre, axis=1, keepdims=True) * (1.0 / width)
        r = lax.rsqrt(var + EPS)
        inv[m] = jnp.broadcast_to(r, (rows, 128))
        normed[m] = (centre * r).astype(BF)
        ys[m] = dot_nt(normed[m], wout[...])
        y_copy(m).start()
        return 0

    lax.fori_loop(0, members, forward, 0)

    def turn(m, _):
        at = pl.ds(pl.multiple_of(m * rows, rows), rows)
        agg_x[:, at] = agg[m].T
        normed_x[:, at] = normed[m].T
        around = jnp.concatenate([halo[m, 0:HALO], lat[m], halo[m, HALO:2 * HALO]], axis=0)
        lat_x[:, pl.ds(pl.multiple_of(m * ext, ext), ext)] = around.T
        return 0

    lax.fori_loop(0, members, turn, 0)

    def y_wait(m, _):
        y_copy(m).wait()
        return 0

    lax.fori_loop(0, members, y_wait, 0)

    total = 2 * members

    def head(m, _):
        y = ys[m]
        miss = y - truth[...]
        pair = jnp.zeros_like(y)
        for o in range(total):
            diff = y - ys[o]
            pair = pair + diff * lax.rsqrt(diff * diff + SMOOTH)
        grad = miss * lax.rsqrt(miss * miss + SMOOTH) * (1.0 / total)
        dy = (area[...] * (grad - (FAIR / (total * (total - 1))) * pair)).astype(BF)
        dys[m] = dy
        dn = dot(dy, wout[...])
        nh = normed[m].astype(F32)
        m1 = jnp.sum(dn, axis=1, keepdims=True) * (1.0 / width)
        m2 = jnp.sum(dn * nh, axis=1, keepdims=True) * (1.0 / width)
        dh[m] = (inv[m][:, 0:1] * (dn - m1 - nh * m2)).astype(BF)
        return 0

    lax.fori_loop(0, members, head, 0)

    halves = []
    left = pl.ds(0, 512)
    at = 0
    for part, held in ((part_mix, held_mix), (part_tgt, held_tgt), (part_src, held_src)):
        wide = part.shape[-1]
        halves.append(Half(place, wire, part, held, left, True, bufs[at:at + 6], bufs[at + 6]))
        halves.append(Half(place, wire, part, held, pl.ds(512, wide - 512), False,
                           bufs[at + 7:at + 13], bufs[at + 13]))
        at += 14
    mix_l, mix_r, tgt_l, tgt_r, src_l, src_r = halves

    def product(turned, right):
        return dot(turned[...], right.reshape(-1, right.shape[-1])).astype(BF)

    def mix_grad(cols):
        put(part_mix, product(agg_x, dh[:, :, cols]), cols)

    columns(mix_grad, 0, 2)
    mix_l.start()
    columns(mix_grad, 2, 4)
    put(part_mix, product(normed_x, dys[...]), pl.ds(width, FP))
    mix_r.start()

    def mix_back(cols):
        dagg = (0.125 * dot_nt(dh[...].reshape(flat, width), wmix[cols, :])).astype(BF)
        dagg = dagg.reshape(members, rows, CW)
        tgt[:, :, cols] = dagg
        dq[:, :, cols] = dagg * slope_sum[:, :, cols]

    columns(mix_back)

    def tgt_grad(cols):
        put(part_tgt, product(grid_x, dq[:, :, cols]), cols)

    columns(tgt_grad, 0, 2)
    tgt_l.start()
    mix_l.s1()
    columns(tgt_grad, 2, 4)
    tgt_r.start()
    mix_r.s1()

    def spread(m):
        def column(cols):
            d = tgt[m, :, cols]
            edges = [slope[m, k, :, cols] * d for k in range(nbrs)]
            got = dot(pick_t[...], jnp.concatenate(edges, axis=0)) + dot(hits_t[...], d)
            dpe[m, :, cols] = got.astype(BF)

        columns(column)
        for one in rim_copies(m):
            one.start()

    spread(0)
    tgt_l.s1()
    mix_l.s2()
    mix_r.s2()
    tgt_r.s1()
    spread(1)
    mix_l.s3()
    mix_r.s3()
    spread(2)
    tgt_l.s2()
    tgt_r.s2()
    mix_l.s4()
    mix_r.s4()
    spread(3)
    tgt_l.s3()
    tgt_r.s3()
    mix_l.s5()
    mix_r.s5()

    def src_grad(cols):
        put(part_src, product(lat_x, dpe[:, :, cols]), cols)

    columns(src_grad, 0, 2)
    src_l.start()
    tgt_l.s4()
    tgt_r.s4()
    columns(src_grad, 2, 4)
    src_r.start()
    src_l.s1()

    def grid_back(cols):
        got = dot_nt(dq[...].reshape(flat, width), wtgt[cols, :]).reshape(members, rows, CW)
        d_grid[:, :, cols] = (dh[:, :, cols].astype(F32) + got).astype(BF)

    columns(grid_back, 0, 2)
    src_r.s1()
    tgt_l.s5()
    tgt_r.s5()
    columns(grid_back, 2, 4)
    src_l.s2()
    src_r.s2()
    o_mix[:, 0:512] = mix_l.s6(scale)
    last = mix_r.s6(scale)
    o_mix[:, 512:width] = last[:, 0:width - 512]
    o_out[...] = last[:, width - 512:width - 512 + fields]

    def sum_rims(m, _):
        for one in rim_copies(m):
            one.wait()
        dq[m] = (dpe[m, HALO:HALO + rows].astype(F32) + rims[m].astype(F32)).astype(BF)
        return 0

    lax.fori_loop(0, members, sum_rims, 0)

    def latent_back(cols):
        got = dot_nt(dq[...].reshape(flat, width), wsrc[cols, :]).reshape(members, rows, CW)
        d_latent[:, :, cols] = got.astype(BF)

    src_l.s3()
    src_r.s3()
    columns(latent_back, 0, 2)
    src_l.s4()
    src_r.s4()
    columns(latent_back, 2, 4)
    src_l.s5()
    src_r.s5()
    o_tgt[:, 0:512] = tgt_l.s6(scale)
    o_tgt[:, 512:width] = tgt_r.s6(scale)
    o_src[:, 0:512] = src_l.s6(scale)
    o_src[:, 512:width] = src_r.s6(scale)


def hand_over(arrays):
    count = len(arrays)

    def move(*refs):
        sems = refs[-1]
        moves = [pltpu.make_async_copy(refs[i], refs[count + i], sems.at[i]) for i in range(count)]
        for one in moves:
            one.start()
        for one in moves:
            one.wait()

    anywhere = pl.BlockSpec(memory_space=pl.ANY)
    return pl.pallas_call(
        move,
        out_shape=[jax.ShapeDtypeStruct(a.shape, a.dtype) for a in arrays],
        in_specs=[anywhere] * count,
        out_specs=[anywhere] * count,
        scratch_shapes=[pltpu.SemaphoreType.DMA((count,))],
    )(*arrays)


def on_device(latent, grid_in, w_src, w_tgt, w_mix, w_out, truth, area, nbr, mask):
    members, rows, width = grid_in.shape
    nbrs = nbr.shape[0]
    fields = w_out.shape[1]
    ext = rows + 2 * HALO
    tiles = lax.axis_size("grid")
    count = members * lax.axis_size("member")
    scale = 1.0 / math.sqrt(rows * tiles * count)

    def body_(*refs):
        body(scale, *refs)

    def ring_bufs(cols):
        return ([pltpu.VMEM((2, 2, 2, 16, cols), BF)] * 3 + [pltpu.VMEM((2, 16, cols), BF)] * 3
                + [pltpu.VMEM((3, 16, cols), BF)])

    vm = pl.BlockSpec(memory_space=pltpu.VMEM)
    hbm = pl.BlockSpec(memory_space=pl.ANY)
    sds = jax.ShapeDtypeStruct
    wide = width + FP
    halves = (512, wide - 512, 512, width - 512, 512, width - 512)
    ncopies = 19 * len(halves)
    results = pl.pallas_call(
        body_,
        out_shape=[
            sds((members, rows, width), BF),
            sds((members, rows, width), BF),
            sds((16, width), F32),
            sds((16, width), F32),
            sds((16, width), F32),
            sds((16, fields), F32),
        ],
        in_specs=[vm, vm, hbm, hbm, hbm, vm, vm, vm, vm, vm],
        out_specs=[vm] * 6,
        scratch_shapes=[
            pltpu.VMEM((width, width), BF),
            pltpu.VMEM((width, width), BF),
            pltpu.VMEM((width, width), BF),
            pltpu.VMEM((FP, width), BF),
            pltpu.VMEM((FP, rows), F32),
            pltpu.VMEM((rows, FP), F32),
            pltpu.VMEM((nbrs, rows, ext), BF),
            pltpu.VMEM((ext, nbrs * rows), BF),
            pltpu.VMEM((rows, ext), BF),
            pltpu.VMEM((ext, rows), BF),
            pltpu.VMEM((nbrs, rows, 128), BF),
            pltpu.VMEM((members, ext, width), BF),
            pltpu.VMEM((members, rows, width), BF),
            pltpu.VMEM((members, nbrs, rows, width), BF),
            pltpu.VMEM((members, rows, width), BF),
            pltpu.VMEM((members, rows, width), BF),
            pltpu.VMEM((members, rows, width), BF),
            pltpu.VMEM((members, rows, 128), F32),
            pltpu.VMEM((2 * members, rows, FP), F32),
            pltpu.VMEM((members, rows, FP), BF),
            pltpu.VMEM((members, rows, width), BF),
            pltpu.VMEM((members, rows, width), BF),
            pltpu.VMEM((members, ext, width), BF),
            pltpu.VMEM((width, members * rows), BF),
            pltpu.VMEM((width, members * rows), BF),
            pltpu.VMEM((width, members * rows), BF),
            pltpu.VMEM((width, members * ext), BF),
            pltpu.VMEM((members, 2 * HALO, width), BF),
            pltpu.VMEM((members, 2 * HALO, width), BF),
            pltpu.VMEM((NC, NY, NX, NZ, 16, width), BF),
            pltpu.VMEM((NC, NY, NX, NZ, 16, width), BF),
            pltpu.VMEM((NC, NY, NX, NZ, 16, wide), BF),
            pltpu.VMEM((NY, NX, NZ, 16, width), BF),
            pltpu.VMEM((NY, NX, NZ, 16, width), BF),
            pltpu.VMEM((NY, NX, NZ, 16, wide), BF),
            *[buf for cols in halves for buf in ring_bufs(cols)],
            pltpu.SemaphoreType.DMA((ncopies,)),
            pltpu.SemaphoreType.DMA((ncopies,)),
            pltpu.SemaphoreType.DMA((2, members)),
            pltpu.SemaphoreType.DMA((2, members)),
            pltpu.SemaphoreType.DMA((2, members)),
            pltpu.SemaphoreType.DMA((2, members)),
            pltpu.SemaphoreType.DMA((members,)),
            pltpu.SemaphoreType.DMA((members,)),
            pltpu.SemaphoreType.DMA((3,)),
        ],
        compiler_params=pltpu.CompilerParams(
            collective_id=0, has_side_effects=True, vmem_limit_bytes=63 * 2**20
        ),
        cost_estimate=pl.CostEstimate(flops=40 * 10**9, bytes_accessed=30 * 10**6, transcendentals=0),
    )(latent, grid_in, w_src, w_tgt, w_mix, w_out.T, truth, area.reshape(1, rows), nbr, mask)
    return hand_over(results)


def solution(mesh):
    in_specs = (
        P("member", "grid", None), P("member", "grid", None), P(), P(), P(), P(),
        P(None, "grid"), P("grid"), P(None, "grid"), P(None, "grid"),
    )
    out_specs = (
        P("member", "grid", None), P("member", "grid", None),
        P("grid", None), P("grid", None), P("grid", None), P("grid", None),
    )
    return jax.shard_map(
        on_device, mesh=mesh, in_specs=in_specs, out_specs=out_specs, check_vma=False
    )
```

time: 1870 us -> 160 us (0.09)
  waiting for transfers between devices: 1490 us -> 0 us
  matrix products: 248 us -> 0 us
  Pallas kernels: 0 us -> 159 us
  local copies, waits for them, and re-layouts: 77.4 us -> 0 us
    unnamed x8 -> x0, waiting for transfers between devices: 1000 us -> none
    reduce_scatter x1 -> x0, waiting for transfers between devices: 315 us -> none  [on_device(): lax.psum_scatter(summed[3], 'grid', scatter_dimension=0, tiled=True)]
    dot_general x60 -> x0, matrix products: 248 us -> none  [the longest x16 97.6 us: backward_step(): jnp.einsum('se,med->msd', picker, proj_ext, preferred_element_type=jnp.fl...]
    psum x1 -> x0, waiting for transfers between devices: 171 us -> none  [on_device(): lax.psum(g_src.astype(jnp.bfloat16), 'member').astype(jnp.float32)]
    pallas_call x0 -> x2, Pallas kernels: none -> 159 us  [the longest x1 88.5 us: on_device(): pl.pallas_call(body_, out_shape=[sds((members, rows, width), BF), sds((me...]
    while x65 -> x0, local copies, waits for them, and re-layouts: 36.5 us -> none
    eq x32 -> x0, local copies, waits for them, and re-layouts: 22.2 us -> none  [the longest x16 11.1 us: forward_step(): picker = (index[:, None] == columns[None, :]).astype(jnp.bfloat16)]
  transfers between devices with their start and end apart: 9 -> 0, of which waited for: 8 -> 0; matrix products, arithmetic and copies ran while one was open for 2% -> 0% of each run, Pallas kernels for 0% -> 0%
where the time goes in v1:
time: 160 us
  Pallas kernels  159 us (99%)
    pallas_call x1, Pallas kernels, on_device(): pl.pallas_call(body_, out_shape=[sds((members, rows, width), BF), sds((me...  88.5 us
    pallas_call x1, Pallas kernels, hand_over(): pl.pallas_call(move, out_shape=[jax.ShapeDtypeStruct(a.shape, a.dtype) fo...  70.9 us

profile of v1, /device:TPU:0, one launch (start us, length us, event | category | flops | bytes accessed | tf_op | source)
XLA Modules:
  0.0 160.1 jit_solution(12411441767985787285)
XLA Ops:
  0.6 88.5 %shard_map.145 = (bf16[4,128,1024]{2,1,0:T(8,128)(2,1)}, bf16[4,128,1024]{2,1,0:T(8,128)(2,1)}, f32[16,1024]{1,0:T(8,128)}, f32[16,1024]{1,0:T(8,128)}, f32[16,1024]{1,0:T(8,128)}, /*index=5*/f32[16,100]{1,0:T(8,128)}) custom-call(bf16[4,128,1024]{2,1,0:T(8,128)(2,1)} %refs_0_.1, bf16[4,128,1024]{2,1,0:T(8,128)(2,1)} %refs_1_.1, bf16[1024,1024]{1,0:T(8,128)(2,1)} %refs_2_.1, ...), custom_call_target="tpu_custom_call" | custom-call | flops 40000000000 | bytes 30000000 | tf_op jit(solution)/shard_map/pallas_call | solution.py:551
  89.2 70.9 %shard_map.146 = (bf16[4,128,1024]{2,1,0:T(8,128)(2,1)}, bf16[4,128,1024]{2,1,0:T(8,128)(2,1)}, f32[16,1024]{1,0:T(8,128)}, f32[16,1024]{1,0:T(8,128)}, f32[16,1024]{1,0:T(8,128)}, /*index=5*/f32[16,100]{1,0:T(8,128)}) custom-call(bf16[4,128,1024]{2,1,0:T(8,128)(2,1)} %get-tuple-element.12.refs_0_, bf16[4,128,1024]{2,1,0:T(8,128)(2,1)} %get-tuple-element.13.refs_1_, ...), custom_call_target="tpu_custom_call" | custom-call | tf_op jit(solution)/shard_map/pallas_call | solution.py:520

commit v2 on v1

--- a/solution.py
+++ b/solution.py
@@ -14,7 +14,7 @@
 BF = jnp.bfloat16
 F32 = jnp.float32
 MESH = pl.DeviceIdType.MESH
-CW = 256
+CW = 512
 NY, NX, NZ, NC = 4, 4, 2, 2
 FP = 128
 
@@ -110,45 +110,48 @@
 
 
 class Half:
-    def __init__(self, place, wire, part, held, cols, y_first, bufs, zbuf):
-        self.place, self.wire, self.zbuf, self.cols = place, wire, zbuf, cols
-        self.part, self.held = part, held
-        y, x = place.y, place.x
+    def __init__(self, place, wire, part, cols, y_first, cross_first, bufs):
+        self.place, self.wire, self.cols, self.part = place, wire, cols, part
+        self.cross_first = cross_first
+        self.held, self.zbuf = bufs[6:]
+        y, x, c = place.y, place.x, place.c
+        cc = c if cross_first else slice(None)
 
         def wide_y(d, h):
-            return held.at[d, pl.ds(2 * h, 2), :, :, cols]
+            return part.at[d, pl.ds(2 * h, 2), :, cc, :, cols]
 
         def wide_x(d, h):
-            return held.at[pl.ds(2 * h, 2), d, :, :, cols]
+            return part.at[pl.ds(2 * h, 2), d, :, cc, :, cols]
 
         def thin_x(d, h):
-            return held.at[y, d, h, :, cols]
+            return part.at[y, d, h, cc, :, cols]
 
         def thin_y(d, h):
-            return held.at[d, x, h, :, cols]
+            return part.at[d, x, h, cc, :, cols]
 
         on_y, on_x = (y, place.y_ring), (x, place.x_ring)
         if y_first:
             self.one = Ring(wire, *on_y, wide_y, *bufs[:3])
-            self.two = Ring(wire, *on_x, thin_x, *bufs[3:])
+            self.two = Ring(wire, *on_x, thin_x, *bufs[3:6])
         else:
             self.one = Ring(wire, *on_x, wide_x, *bufs[:3])
-            self.two = Ring(wire, *on_y, thin_y, *bufs[3:])
+            self.two = Ring(wire, *on_y, thin_y, *bufs[3:6])
 
     def start(self):
-        cols = self.cols
-        self.cross = [self.wire.copy(self.part.at[1 - self.place.c, yy, :, :, :, cols],
-                                     self.held.at[yy, :, :, :, cols], self.place.core) for yy in range(NY)]
-        for one in self.cross:
-            one.start()
+        if not self.cross_first:
+            self.one.start()
+            return
+        self.cross = self.wire.copy(self.part.at[:, :, :, 1 - self.place.c, :, self.cols], self.held,
+                                    self.place.core)
+        self.cross.start()
 
     def s1(self):
-        for one in self.cross:
-            one.wait()
-        cols = self.cols
+        if not self.cross_first:
+            return
+        self.cross.wait()
 
         def add(yy, _):
-            add_into(self.held.at[yy, :, :, :, cols], self.part.at[self.place.c, yy, :, :, :, cols])
+            add_into(self.part.at[yy, :, :, self.place.c, :, self.cols], self.held.at[yy])
             return 0
 
         lax.fori_loop(0, NY, add, 0)
@@ -167,18 +170,35 @@
     def s5(self):
         self.two.finish()
         p = self.place
-        mine = self.held.at[p.y, p.x]
-        self.last = [self.wire.copy(mine.at[p.z, :, self.cols], self.zbuf.at[0], p.mate),
-                     self.wire.copy(mine.at[1 - p.z, :, self.cols], self.zbuf.at[1], p.z_far),
-                     self.wire.copy(mine.at[1 - p.z, :, self.cols], self.zbuf.at[2], p.z_both)]
+        if self.cross_first:
+            self.to_z()
+            return
+        mine = self.part.at[p.y, p.x]
+        self.cross = self.wire.copy(mine.at[:, 1 - p.c, :, self.cols], self.held, p.core)
+        self.cross.start()
+
+    def s6(self):
+        if self.cross_first:
+            return
+        p = self.place
+        self.cross.wait()
+        add_into(self.part.at[p.y, p.x, :, p.c, :, self.cols], self.held)
+        self.to_z()
+
+    def to_z(self):
+        p = self.place
+        mine, far = self.part.at[p.y, p.x, p.z, p.c], self.part.at[p.y, p.x, 1 - p.z, p.c]
+        self.last = [self.wire.copy(mine.at[:, self.cols], self.zbuf.at[0], p.mate),
+                     self.wire.copy(far.at[:, self.cols], self.zbuf.at[1], p.z_far),
+                     self.wire.copy(far.at[:, self.cols], self.zbuf.at[2], p.z_both)]
         for one in self.last:
             one.start()
 
-    def s6(self, scale):
+    def s7(self, scale):
         p = self.place
         for one in self.last:
             one.wait()
-        total = self.held[p.y, p.x, p.z, :, self.cols].astype(F32)
+        total = self.part[p.y, p.x, p.z, p.c, :, self.cols].astype(F32)
         for k in range(3):
             total = total + self.zbuf[k].astype(F32)
         return total * scale
@@ -186,7 +206,7 @@
 
 def put(part, block, cols):
     for b in range(NY * NX * NZ * NC):
-        part[b % 2, b // 16, (b // 4) % 4, (b // 2) % 2, :, cols] = block[b * 16:(b + 1) * 16]
+        part[b // 16, (b // 4) % 4, (b // 2) % 2, b % 2, :, cols] = block[b * 16:(b + 1) * 16]
 
 
 def body(scale, lat, grid, wsrc_in, wtgt_in, wmix_in, wout_in, truth_in, area_in, nbr, mask,
@@ -194,7 +214,7 @@
          wsrc, wtgt, wmix, wout, truth, area,
          pick, pick_t, hits, hits_t, maskb, proj, tgt, slope, slope_sum, agg, normed, inv, ys, dys, dh, dq, dpe,
          agg_x, normed_x, grid_x, lat_x,
-         halo, rims, part_src, part_tgt, part_mix, held_src, held_tgt, held_mix, *rest):
+         halo, rims, part_src, part_tgt, part_mix, *rest):
     send_sem, recv_sem, halo_send, halo_recv, rim_send, rim_recv, y_send, y_recv, load_sem = rest[-9:]
     bufs = rest[:-9]
     members, rows, width = grid.shape
@@ -300,7 +320,7 @@
     lax.fori_loop(0, members, turn_grid, 0)
     loads[2].wait()
 
-    gb = 16
+    gb = 32
 
     def forward(m, _):
         for one in halo_copies(m):
@@ -309,28 +329,28 @@
         proj[m, 0:HALO] = edge[0:HALO]
         proj[m, HALO + rows:ext] = edge[HALO:2 * HALO]
 
-        def column(cols):
-            table = proj[m, :, cols]
-            linear = dot(hits[...], table) + count * tgt[m, :, cols].astype(F32)
-            for at in range(0, rows, gb):
-                got = dot(pick[:, at:at + gb, :].reshape(nbrs * gb, ext), table).astype(BF)
-                got = got.reshape(nbrs, gb, CW)
+        linear = dot(hits[...], proj[m]) + count * tgt[m].astype(F32)
+        for at in range(0, rows, gb):
+            got = dot(pick[:, at:at + gb, :].reshape(nbrs * gb, ext), proj[m]).astype(BF)
+            got = got.reshape(nbrs, gb, width)
+            for c in range(0, width, 256):
+                cols = slice(c, c + 256)
                 base = tgt[m, at:at + gb, cols]
                 acc = None
                 acc_s = None
                 for k in range(nbrs):
                     on = maskb[k, at:at + gb, :]
-                    u = got[k] + jnp.concatenate([on] * (CW // 128), axis=1) * base
+                    u = got[k, :, cols] + jnp.concatenate([on, on], axis=1) * base
                     t = jnp.tanh(u)
                     p = u * t
                     s = (t + u) - t * p
                     acc = p if k == 0 else acc + p
                     acc_s = s if k == 0 else acc_s + s
                     slope[m, k, at:at + gb, cols] = s
-                agg[m, at:at + gb, cols] = (0.25 * (linear[at:at + gb] + acc.astype(F32))).astype(BF)
+                total = linear[at:at + gb, cols] + acc.astype(F32)
+                agg[m, at:at + gb, cols] = (0.25 * total).astype(BF)
                 slope_sum[m, at:at + gb, cols] = (acc_s.astype(F32) + count[at:at + gb]).astype(BF)
 
-        columns(column)
         h = grid[m].astype(F32) + dot(agg[m], wmix[...])
         mean = jnp.sum(h, axis=1, keepdims=True) * (1.0 / width)
         centre = h - mean
@@ -383,13 +403,11 @@
 
     halves = []
     left = pl.ds(0, 512)
-    at = 0
-    for part, held in ((part_mix, held_mix), (part_tgt, held_tgt), (part_src, held_src)):
+    for i, part in enumerate((part_mix, part_tgt, part_src)):
         wide = part.shape[-1]
-        halves.append(Half(place, wire, part, held, left, True, bufs[at:at + 6], bufs[at + 6]))
-        halves.append(Half(place, wire, part, held, pl.ds(512, wide - 512), False,
-                           bufs[at + 7:at + 13], bufs[at + 13]))
-        at += 14
+        at = 16 * i
+        halves.append(Half(place, wire, part, left, i != 1, True, bufs[at:at + 8]))
+        halves.append(Half(place, wire, part, pl.ds(512, wide - 512), i == 1, False, bufs[at + 8:at + 16]))
     mix_l, mix_r, tgt_l, tgt_r, src_l, src_r = halves
 
     def product(turned, right):
@@ -398,11 +416,11 @@
     def mix_grad(cols):
         put(part_mix, product(agg_x, dh[:, :, cols]), cols)
 
-    columns(mix_grad, 0, 2)
-    mix_l.start()
-    columns(mix_grad, 2, 4)
+    columns(mix_grad, 1, 2)
     put(part_mix, product(normed_x, dys[...]), pl.ds(width, FP))
     mix_r.start()
+    columns(mix_grad, 0, 1)
+    mix_l.start()
 
     def mix_back(cols):
         dagg = (0.125 * dot_nt(dh[...].reshape(flat, width), wmix[cols, :])).astype(BF)
@@ -415,18 +433,19 @@
     def tgt_grad(cols):
         put(part_tgt, product(grid_x, dq[:, :, cols]), cols)
 
-    columns(tgt_grad, 0, 2)
+    columns(tgt_grad, 1, 2)
+    tgt_r.start()
+    columns(tgt_grad, 0, 1)
     tgt_l.start()
     mix_l.s1()
-    columns(tgt_grad, 2, 4)
-    tgt_r.start()
-    mix_r.s1()
 
     def spread(m):
         def column(cols):
             d = tgt[m, :, cols]
-            edges = [slope[m, k, :, cols] * d for k in range(nbrs)]
-            got = dot(pick_t[...], jnp.concatenate(edges, axis=0)) + dot(hits_t[...], d)
+            for k in range(nbrs):
+                slope[m, k, :, cols] = slope[m, k, :, cols] * d
+            edges = slope[m, :, :, cols].reshape(nbrs * rows, CW)
+            got = dot(pick_t[...], edges) + dot(hits_t[...], d)
             dpe[m, :, cols] = got.astype(BF)
 
         columns(column)
@@ -434,48 +453,48 @@
             one.start()
 
     spread(0)
+    mix_r.s2()
     tgt_l.s1()
+    spread(1)
     mix_l.s2()
-    mix_r.s2()
-    tgt_r.s1()
-    spread(1)
+    mix_r.s3()
+    tgt_r.s2()
+    spread(2)
     mix_l.s3()
-    mix_r.s3()
-    spread(2)
+    mix_r.s4()
     tgt_l.s2()
-    tgt_r.s2()
+    spread(3)
     mix_l.s4()
-    mix_r.s4()
-    spread(3)
+    mix_r.s5()
+    tgt_r.s3()
     tgt_l.s3()
-    tgt_r.s3()
-    mix_l.s5()
-    mix_r.s5()
 
     def src_grad(cols):
         put(part_src, product(lat_x, dpe[:, :, cols]), cols)
 
-    columns(src_grad, 0, 2)
-    src_l.start()
+    columns(src_grad, 1, 2)
+    src_r.start()
+    mix_l.s5()
+    mix_r.s6()
     tgt_l.s4()
     tgt_r.s4()
-    columns(src_grad, 2, 4)
-    src_r.start()
-    src_l.s1()
+    columns(src_grad, 0, 1)
+    src_l.start()
+    tgt_l.s5()
+    tgt_r.s5()
 
     def grid_back(cols):
         got = dot_nt(dq[...].reshape(flat, width), wtgt[cols, :]).reshape(members, rows, CW)
         d_grid[:, :, cols] = (dh[:, :, cols].astype(F32) + got).astype(BF)
 
-    columns(grid_back, 0, 2)
-    src_r.s1()
-    tgt_l.s5()
-    tgt_r.s5()
-    columns(grid_back, 2, 4)
+    columns(grid_back, 0, 1)
+    src_l.s1()
+    tgt_r.s6()
+    columns(grid_back, 1, 2)
+    src_r.s2()
     src_l.s2()
-    src_r.s2()
-    o_mix[:, 0:512] = mix_l.s6(scale)
-    last = mix_r.s6(scale)
+    o_mix[:, 0:512] = mix_l.s7(scale)
+    last = mix_r.s7(scale)
     o_mix[:, 512:width] = last[:, 0:width - 512]
     o_out[...] = last[:, width - 512:width - 512 + fields]
 
@@ -491,18 +510,19 @@
         got = dot_nt(dq[...].reshape(flat, width), wsrc[cols, :]).reshape(members, rows, CW)
         d_latent[:, :, cols] = got.astype(BF)
 
+    columns(latent_back, 0, 1)
     src_l.s3()
     src_r.s3()
-    columns(latent_back, 0, 2)
+    columns(latent_back, 1, 2)
     src_l.s4()
     src_r.s4()
-    columns(latent_back, 2, 4)
     src_l.s5()
     src_r.s5()
-    o_tgt[:, 0:512] = tgt_l.s6(scale)
-    o_tgt[:, 512:width] = tgt_r.s6(scale)
-    o_src[:, 0:512] = src_l.s6(scale)
-    o_src[:, 512:width] = src_r.s6(scale)
+    src_r.s6()
+    o_tgt[:, 0:512] = tgt_l.s7(scale)
+    o_tgt[:, 512:width] = tgt_r.s7(scale)
+    o_src[:, 0:512] = src_l.s7(scale)
+    o_src[:, 512:width] = src_r.s7(scale)
 
 
 def hand_over(arrays):
@@ -520,7 +540,7 @@
     return pl.pallas_call(
         move,
         out_shape=[jax.ShapeDtypeStruct(a.shape, a.dtype) for a in arrays],
-        in_specs=[anywhere] * count,
+        in_specs=[pl.BlockSpec(memory_space=pltpu.VMEM)] * count,
         out_specs=[anywhere] * count,
         scratch_shapes=[pltpu.SemaphoreType.DMA((count,))],
     )(*arrays)
@@ -538,16 +558,18 @@
     def body_(*refs):
         body(scale, *refs)
 
-    def ring_bufs(cols):
-        return ([pltpu.VMEM((2, 2, 2, 16, cols), BF)] * 3 + [pltpu.VMEM((2, 16, cols), BF)] * 3
-                + [pltpu.VMEM((3, 16, cols), BF)])
+    def half_bufs(cols, cross_first):
+        both = () if cross_first else (NC,)
+        held = (NY, NX, NZ, 16, cols) if cross_first else (NZ, 16, cols)
+        return ([pltpu.VMEM((2, 2, 2, *both, 16, cols), BF)] * 3 + [pltpu.VMEM((2, *both, 16, cols), BF)] * 3
+                + [pltpu.VMEM(held, BF), pltpu.VMEM((3, 16, cols), BF)])
 
     vm = pl.BlockSpec(memory_space=pltpu.VMEM)
     hbm = pl.BlockSpec(memory_space=pl.ANY)
     sds = jax.ShapeDtypeStruct
     wide = width + FP
     halves = (512, wide - 512, 512, width - 512, 512, width - 512)
-    ncopies = 19 * len(halves)
+    ncopies = 16 * len(halves)
     results = pl.pallas_call(
         body_,
         out_shape=[
@@ -590,13 +612,10 @@
             pltpu.VMEM((width, members * ext), BF),
             pltpu.VMEM((members, 2 * HALO, width), BF),
             pltpu.VMEM((members, 2 * HALO, width), BF),
-            pltpu.VMEM((NC, NY, NX, NZ, 16, width), BF),
-            pltpu.VMEM((NC, NY, NX, NZ, 16, width), BF),
-            pltpu.VMEM((NC, NY, NX, NZ, 16, wide), BF),
-            pltpu.VMEM((NY, NX, NZ, 16, width), BF),
-            pltpu.VMEM((NY, NX, NZ, 16, width), BF),
-            pltpu.VMEM((NY, NX, NZ, 16, wide), BF),
-            *[buf for cols in halves for buf in ring_bufs(cols)],
+            pltpu.VMEM((NY, NX, NZ, NC, 16, width), BF),
+            pltpu.VMEM((NY, NX, NZ, NC, 16, width), BF),
+            pltpu.VMEM((NY, NX, NZ, NC, 16, wide), BF),
+            *[buf for i, cols in enumerate(halves) for buf in half_bufs(cols, i % 2 == 0)],
             pltpu.SemaphoreType.DMA((ncopies,)),
             pltpu.SemaphoreType.DMA((ncopies,)),
             pltpu.SemaphoreType.DMA((2, members)),

time: 160 us -> 99.7 us (0.62)
  Pallas kernels: 159 us -> 98.3 us
    pallas_call x1, Pallas kernels: 70.9 us -> 2.99 us  [hand_over(): pl.pallas_call(move, out_shape=[jax.ShapeDtypeStruct(a.shape, a.dtype) fo...]
    pallas_call x1, Pallas kernels: 88.5 us -> 95.4 us  [on_device(): pl.pallas_call(body_, out_shape=[sds((members, rows, width), BF), sds((me...]
where the time goes in v2:
time: 99.7 us; the launch traced here: 99.1 us
  Pallas kernels  98.3 us (99%)
    pallas_call x1, Pallas kernels, on_device(): pl.pallas_call(body_, out_shape=[sds((members, rows, width), BF), sds((me...  95.4 us
    pallas_call x1, Pallas kernels, hand_over(): pl.pallas_call(move, out_shape=[jax.ShapeDtypeStruct(a.shape, a.dtype) fo...  2.99 us

profile of v2, /device:TPU:0, one launch (start us, length us, event | category | flops | bytes accessed | tf_op | source)
XLA Modules:
  0.0 99.1 jit_solution(8712158147430522748)
XLA Ops:
  0.6 95.4 %shard_map.145 = (bf16[4,128,1024]{2,1,0:T(8,128)(2,1)}, bf16[4,128,1024]{2,1,0:T(8,128)(2,1)}, f32[16,1024]{1,0:T(8,128)}, f32[16,1024]{1,0:T(8,128)}, f32[16,1024]{1,0:T(8,128)}, /*index=5*/f32[16,100]{1,0:T(8,128)}) custom-call(bf16[4,128,1024]{2,1,0:T(8,128)(2,1)} %refs_0_.1, bf16[4,128,1024]{2,1,0:T(8,128)(2,1)} %refs_1_.1, bf16[1024,1024]{1,0:T(8,128)(2,1)} %refs_2_.1, ...), custom_call_target="tpu_custom_call" | custom-call | flops 40000000000 | bytes 30000000 | tf_op jit(solution)/shard_map/pallas_call | solution.py:573
  96.0 3.0 %shard_map.146 = (bf16[4,128,1024]{2,1,0:T(8,128)(2,1)}, bf16[4,128,1024]{2,1,0:T(8,128)(2,1)}, f32[16,1024]{1,0:T(8,128)}, f32[16,1024]{1,0:T(8,128)}, f32[16,1024]{1,0:T(8,128)}, /*index=5*/f32[16,100]{1,0:T(8,128)}) custom-call(bf16[4,128,1024]{2,1,0:T(8,128)(2,1)} %get-tuple-element.12.refs_0_, bf16[4,128,1024]{2,1,0:T(8,128)(2,1)} %get-tuple-element.13.refs_1_, ...), custom_call_target="tpu_custom_call" | custom-call | tf_op jit(solution)/shard_map/pallas_call | solution.py:540

commit v3 on v1

--- a/solution.py
+++ b/solution.py
@@ -14,7 +14,7 @@
 BF = jnp.bfloat16
 F32 = jnp.float32
 MESH = pl.DeviceIdType.MESH
-CW = 256
+CW = 512
 NY, NX, NZ, NC = 4, 4, 2, 2
 FP = 128
 
@@ -41,8 +41,8 @@
         self.down = (self.me, (t + tiles - 1) % tiles)
         self.mate = (1 - self.me, t)
         self.core = self.at(c=1 - self.c)
-        self.y_ring = (self.at(y=(self.y + 1) % 4), self.at(y=(self.y + 3) % 4))
-        self.x_ring = (self.at(x=(self.x + 1) % 4), self.at(x=(self.x + 3) % 4))
+        self.y_ring = tuple(self.at(y=(self.y + k) % 4) for k in (1, 2, 3))
+        self.x_ring = tuple(self.at(x=(self.x + k) % 4) for k in (1, 2, 3))
         self.z_far = (self.me, self.at(z=1 - self.z)[1])
         self.z_both = (1 - self.me, self.z_far[1])
         self.partners = (self.up, self.down, self.core, *self.y_ring, *self.x_ring,
@@ -75,38 +75,20 @@
     dst[...] = total.astype(BF)
 
 
-class Ring:
-    def __init__(self, wire, p, ring, block, a, b, d):
-        self.wire, self.p, self.ring, self.block = wire, p, ring, block
-        self.a, self.b, self.d = a, b, d
-        self.nxt, self.prv = (p + 1) % 4, (p + 3) % 4
+class Swap:
+    def __init__(self, wire, p, others, block, buf):
+        self.wire, self.p, self.others, self.block, self.buf = wire, p, others, block, buf
 
     def start(self):
-        w, (plus, minus), block = self.wire, self.ring, self.block
-        opp = (self.p + 2) % 4
-        self.first = [w.copy(block(opp, 0), self.a.at[0], plus),
-                      w.copy(block(opp, 1), self.a.at[1], minus)]
-        self.second = [w.copy(block(self.nxt, 1), self.b.at[0], plus),
-                       w.copy(block(self.prv, 0), self.b.at[1], minus)]
-        for one in self.first + self.second:
+        self.moves = [self.wire.copy(self.block((self.p + k) % 4), self.buf.at[k - 1], self.others[k - 1])
+                      for k in (1, 3, 2)]
+        for one in self.moves:
             one.start()
 
-    def middle(self):
-        w, (plus, minus), block = self.wire, self.ring, self.block
-        self.third = [w.copy(block(self.nxt, 0), self.d.at[0], plus),
-                      w.copy(block(self.prv, 1), self.d.at[1], minus)]
-        self.first[0].wait()
-        add_into(block(self.nxt, 0), self.a.at[0])
-        self.third[0].start()
-        self.first[1].wait()
-        add_into(block(self.prv, 1), self.a.at[1])
-        self.third[1].start()
-
     def finish(self):
-        for one in self.second + self.third:
+        for one in self.moves:
             one.wait()
-        add_into(self.block(self.p, 0), self.b.at[1], self.d.at[0])
-        add_into(self.block(self.p, 1), self.b.at[0], self.d.at[1])
+        add_into(self.block(self.p), *[self.buf.at[k] for k in range(3)])
 
 
 class Half:
@@ -115,36 +97,22 @@
         self.part, self.held = part, held
         y, x = place.y, place.x
 
-        def wide_y(d, h):
-            return held.at[d, pl.ds(2 * h, 2), :, :, cols]
-
-        def wide_x(d, h):
-            return held.at[pl.ds(2 * h, 2), d, :, :, cols]
-
-        def thin_x(d, h):
-            return held.at[y, d, h, :, cols]
-
-        def thin_y(d, h):
-            return held.at[d, x, h, :, cols]
-
         on_y, on_x = (y, place.y_ring), (x, place.x_ring)
         if y_first:
-            self.one = Ring(wire, *on_y, wide_y, *bufs[:3])
-            self.two = Ring(wire, *on_x, thin_x, *bufs[3:])
+            self.one = Swap(wire, *on_y, lambda d: held.at[d, :, :, :, cols], bufs[0])
+            self.two = Swap(wire, *on_x, lambda d: held.at[y, d, :, :, cols], bufs[1])
         else:
-            self.one = Ring(wire, *on_x, wide_x, *bufs[:3])
-            self.two = Ring(wire, *on_y, thin_y, *bufs[3:])
+            self.one = Swap(wire, *on_x, lambda d: held.at[:, d, :, :, cols], bufs[0])
+            self.two = Swap(wire, *on_y, lambda d: held.at[d, x, :, :, cols], bufs[1])
 
     def start(self):
         cols = self.cols
-        self.cross = [self.wire.copy(self.part.at[1 - self.place.c, yy, :, :, :, cols],
-                                     self.held.at[yy, :, :, :, cols], self.place.core) for yy in range(NY)]
-        for one in self.cross:
-            one.start()
+        self.cross = self.wire.copy(self.part.at[1 - self.place.c, :, :, :, :, cols],
+                                    self.held.at[:, :, :, :, cols], self.place.core)
+        self.cross.start()
 
     def s1(self):
-        for one in self.cross:
-            one.wait()
+        self.cross.wait()
         cols = self.cols
 
         def add(yy, _):
@@ -155,16 +123,10 @@
         self.one.start()
 
     def s2(self):
-        self.one.middle()
-
-    def s3(self):
         self.one.finish()
         self.two.start()
 
-    def s4(self):
-        self.two.middle()
-
-    def s5(self):
+    def s3(self):
         self.two.finish()
         p = self.place
         mine = self.held.at[p.y, p.x]
@@ -174,7 +136,7 @@
         for one in self.last:
             one.start()
 
-    def s6(self, scale):
+    def s4(self, scale):
         p = self.place
         for one in self.last:
             one.wait()
@@ -300,7 +262,7 @@
     lax.fori_loop(0, members, turn_grid, 0)
     loads[2].wait()
 
-    gb = 16
+    gb = 32
 
     def forward(m, _):
         for one in halo_copies(m):
@@ -309,28 +271,28 @@
         proj[m, 0:HALO] = edge[0:HALO]
         proj[m, HALO + rows:ext] = edge[HALO:2 * HALO]
 
-        def column(cols):
-            table = proj[m, :, cols]
-            linear = dot(hits[...], table) + count * tgt[m, :, cols].astype(F32)
-            for at in range(0, rows, gb):
-                got = dot(pick[:, at:at + gb, :].reshape(nbrs * gb, ext), table).astype(BF)
-                got = got.reshape(nbrs, gb, CW)
+        linear = dot(hits[...], proj[m]) + count * tgt[m].astype(F32)
+        for at in range(0, rows, gb):
+            got = dot(pick[:, at:at + gb, :].reshape(nbrs * gb, ext), proj[m]).astype(BF)
+            got = got.reshape(nbrs, gb, width)
+            for c in range(0, width, 256):
+                cols = slice(c, c + 256)
                 base = tgt[m, at:at + gb, cols]
                 acc = None
                 acc_s = None
                 for k in range(nbrs):
                     on = maskb[k, at:at + gb, :]
-                    u = got[k] + jnp.concatenate([on] * (CW // 128), axis=1) * base
+                    u = got[k, :, cols] + jnp.concatenate([on, on], axis=1) * base
                     t = jnp.tanh(u)
                     p = u * t
                     s = (t + u) - t * p
                     acc = p if k == 0 else acc + p
                     acc_s = s if k == 0 else acc_s + s
                     slope[m, k, at:at + gb, cols] = s
-                agg[m, at:at + gb, cols] = (0.25 * (linear[at:at + gb] + acc.astype(F32))).astype(BF)
+                total = linear[at:at + gb, cols] + acc.astype(F32)
+                agg[m, at:at + gb, cols] = (0.25 * total).astype(BF)
                 slope_sum[m, at:at + gb, cols] = (acc_s.astype(F32) + count[at:at + gb]).astype(BF)
 
-        columns(column)
         h = grid[m].astype(F32) + dot(agg[m], wmix[...])
         mean = jnp.sum(h, axis=1, keepdims=True) * (1.0 / width)
         centre = h - mean
@@ -386,10 +348,10 @@
     at = 0
     for part, held in ((part_mix, held_mix), (part_tgt, held_tgt), (part_src, held_src)):
         wide = part.shape[-1]
-        halves.append(Half(place, wire, part, held, left, True, bufs[at:at + 6], bufs[at + 6]))
+        halves.append(Half(place, wire, part, held, left, True, bufs[at:at + 2], bufs[at + 2]))
         halves.append(Half(place, wire, part, held, pl.ds(512, wide - 512), False,
-                           bufs[at + 7:at + 13], bufs[at + 13]))
-        at += 14
+                           bufs[at + 3:at + 5], bufs[at + 5]))
+        at += 6
     mix_l, mix_r, tgt_l, tgt_r, src_l, src_r = halves
 
     def product(turned, right):
@@ -398,9 +360,9 @@
     def mix_grad(cols):
         put(part_mix, product(agg_x, dh[:, :, cols]), cols)
 
-    columns(mix_grad, 0, 2)
+    columns(mix_grad, 0, 1)
     mix_l.start()
-    columns(mix_grad, 2, 4)
+    columns(mix_grad, 1, 2)
     put(part_mix, product(normed_x, dys[...]), pl.ds(width, FP))
     mix_r.start()
 
@@ -415,18 +377,20 @@
     def tgt_grad(cols):
         put(part_tgt, product(grid_x, dq[:, :, cols]), cols)
 
-    columns(tgt_grad, 0, 2)
+    columns(tgt_grad, 0, 1)
     tgt_l.start()
+    columns(tgt_grad, 1, 2)
+    tgt_r.start()
     mix_l.s1()
-    columns(tgt_grad, 2, 4)
-    tgt_r.start()
     mix_r.s1()
 
     def spread(m):
         def column(cols):
             d = tgt[m, :, cols]
-            edges = [slope[m, k, :, cols] * d for k in range(nbrs)]
-            got = dot(pick_t[...], jnp.concatenate(edges, axis=0)) + dot(hits_t[...], d)
+            for k in range(nbrs):
+                slope[m, k, :, cols] = slope[m, k, :, cols] * d
+            edges = slope[m, :, :, cols].reshape(nbrs * rows, CW)
+            got = dot(pick_t[...], edges) + dot(hits_t[...], d)
             dpe[m, :, cols] = got.astype(BF)
 
         columns(column)
@@ -435,47 +399,37 @@
 
     spread(0)
     tgt_l.s1()
+    tgt_r.s1()
+    spread(1)
+    spread(2)
     mix_l.s2()
     mix_r.s2()
-    tgt_r.s1()
-    spread(1)
+    spread(3)
+
+    def src_grad(cols):
+        put(part_src, product(lat_x, dpe[:, :, cols]), cols)
+
+    columns(src_grad, 0, 1)
+    src_l.start()
+    tgt_l.s2()
+    tgt_r.s2()
+    columns(src_grad, 1, 2)
+    src_r.start()
     mix_l.s3()
     mix_r.s3()
-    spread(2)
-    tgt_l.s2()
-    tgt_r.s2()
-    mix_l.s4()
-    mix_r.s4()
-    spread(3)
-    tgt_l.s3()
-    tgt_r.s3()
-    mix_l.s5()
-    mix_r.s5()
-
-    def src_grad(cols):
-        put(part_src, product(lat_x, dpe[:, :, cols]), cols)
-
-    columns(src_grad, 0, 2)
-    src_l.start()
-    tgt_l.s4()
-    tgt_r.s4()
-    columns(src_grad, 2, 4)
-    src_r.start()
     src_l.s1()
 
     def grid_back(cols):
         got = dot_nt(dq[...].reshape(flat, width), wtgt[cols, :]).reshape(members, rows, CW)
         d_grid[:, :, cols] = (dh[:, :, cols].astype(F32) + got).astype(BF)
 
-    columns(grid_back, 0, 2)
+    columns(grid_back, 0, 1)
     src_r.s1()
-    tgt_l.s5()
-    tgt_r.s5()
-    columns(grid_back, 2, 4)
-    src_l.s2()
-    src_r.s2()
-    o_mix[:, 0:512] = mix_l.s6(scale)
-    last = mix_r.s6(scale)
+    columns(grid_back, 1, 2)
+    tgt_l.s3()
+    tgt_r.s3()
+    o_mix[:, 0:512] = mix_l.s4(scale)
+    last = mix_r.s4(scale)
     o_mix[:, 512:width] = last[:, 0:width - 512]
     o_out[...] = last[:, width - 512:width - 512 + fields]
 
@@ -491,18 +445,16 @@
         got = dot_nt(dq[...].reshape(flat, width), wsrc[cols, :]).reshape(members, rows, CW)
         d_latent[:, :, cols] = got.astype(BF)
 
+    columns(latent_back, 0, 1)
+    src_l.s2()
+    columns(latent_back, 1, 2)
+    src_r.s2()
     src_l.s3()
     src_r.s3()
-    columns(latent_back, 0, 2)
-    src_l.s4()
-    src_r.s4()
-    columns(latent_back, 2, 4)
-    src_l.s5()
-    src_r.s5()
-    o_tgt[:, 0:512] = tgt_l.s6(scale)
-    o_tgt[:, 512:width] = tgt_r.s6(scale)
-    o_src[:, 0:512] = src_l.s6(scale)
-    o_src[:, 512:width] = src_r.s6(scale)
+    o_tgt[:, 0:512] = tgt_l.s4(scale)
+    o_tgt[:, 512:width] = tgt_r.s4(scale)
+    o_src[:, 0:512] = src_l.s4(scale)
+    o_src[:, 512:width] = src_r.s4(scale)
 
 
 def hand_over(arrays):
@@ -520,7 +472,7 @@
     return pl.pallas_call(
         move,
         out_shape=[jax.ShapeDtypeStruct(a.shape, a.dtype) for a in arrays],
-        in_specs=[anywhere] * count,
+        in_specs=[pl.BlockSpec(memory_space=pltpu.VMEM)] * count,
         out_specs=[anywhere] * count,
         scratch_shapes=[pltpu.SemaphoreType.DMA((count,))],
     )(*arrays)
@@ -539,15 +491,15 @@
         body(scale, *refs)
 
     def ring_bufs(cols):
-        return ([pltpu.VMEM((2, 2, 2, 16, cols), BF)] * 3 + [pltpu.VMEM((2, 16, cols), BF)] * 3
-                + [pltpu.VMEM((3, 16, cols), BF)])
+        return [pltpu.VMEM((3, 4, 2, 16, cols), BF), pltpu.VMEM((3, 2, 16, cols), BF),
+                pltpu.VMEM((3, 16, cols), BF)]
 
     vm = pl.BlockSpec(memory_space=pltpu.VMEM)
     hbm = pl.BlockSpec(memory_space=pl.ANY)
     sds = jax.ShapeDtypeStruct
     wide = width + FP
     halves = (512, wide - 512, 512, width - 512, 512, width - 512)
-    ncopies = 19 * len(halves)
+    ncopies = 10 * len(halves)
     results = pl.pallas_call(
         body_,
         out_shape=[

time: 160 us -> 85.2 us (0.53)
  Pallas kernels: 159 us -> 83 us
    pallas_call x1, Pallas kernels: 70.9 us -> 2.99 us  [hand_over(): pl.pallas_call(move, out_shape=[jax.ShapeDtypeStruct(a.shape, a.dtype) fo...]
    pallas_call x1, Pallas kernels: 88.5 us -> 80 us  [on_device(): pl.pallas_call(body_, out_shape=[sds((members, rows, width), BF), sds((me...]
where the time goes in v3:
time: 85.2 us; the launch traced here: 83.8 us
  Pallas kernels  83 us (97%)
    pallas_call x1, Pallas kernels, on_device(): pl.pallas_call(body_, out_shape=[sds((members, rows, width), BF), sds((me...  80 us
    pallas_call x1, Pallas kernels, hand_over(): pl.pallas_call(move, out_shape=[jax.ShapeDtypeStruct(a.shape, a.dtype) fo...  2.99 us

profile of v3, /device:TPU:0, one launch (start us, length us, event | category | flops | bytes accessed | tf_op | source)
XLA Modules:
  0.0 83.8 jit_solution(12656514565683643245)
XLA Ops:
  0.6 80.0 %shard_map.145 = (bf16[4,128,1024]{2,1,0:T(8,128)(2,1)}, bf16[4,128,1024]{2,1,0:T(8,128)(2,1)}, f32[16,1024]{1,0:T(8,128)}, f32[16,1024]{1,0:T(8,128)}, f32[16,1024]{1,0:T(8,128)}, /*index=5*/f32[16,100]{1,0:T(8,128)}) custom-call(bf16[4,128,1024]{2,1,0:T(8,128)(2,1)} %refs_0_.1, bf16[4,128,1024]{2,1,0:T(8,128)(2,1)} %refs_1_.1, bf16[1024,1024]{1,0:T(8,128)(2,1)} %refs_2_.1, ...), custom_call_target="tpu_custom_call" | custom-call | flops 40000000000 | bytes 30000000 | tf_op jit(solution)/shard_map/pallas_call | solution.py:503
  80.7 3.0 %shard_map.146 = (bf16[4,128,1024]{2,1,0:T(8,128)(2,1)}, bf16[4,128,1024]{2,1,0:T(8,128)(2,1)}, f32[16,1024]{1,0:T(8,128)}, f32[16,1024]{1,0:T(8,128)}, f32[16,1024]{1,0:T(8,128)}, /*index=5*/f32[16,100]{1,0:T(8,128)}) custom-call(bf16[4,128,1024]{2,1,0:T(8,128)(2,1)} %get-tuple-element.12.refs_0_, bf16[4,128,1024]{2,1,0:T(8,128)(2,1)} %get-tuple-element.13.refs_1_, ...), custom_call_target="tpu_custom_call" | custom-call | tf_op jit(solution)/shard_map/pallas_call | solution.py:472

commit v4 on v3

--- a/solution.py
+++ b/solution.py
@@ -155,7 +155,7 @@
          d_latent, d_grid, o_src, o_tgt, o_mix, o_out,
          wsrc, wtgt, wmix, wout, truth, area,
          pick, pick_t, hits, hits_t, maskb, proj, tgt, slope, slope_sum, agg, normed, inv, ys, dys, dh, dq, dpe,
-         agg_x, normed_x, grid_x, lat_x,
+         agg_x, normed_x, grid_x, lat_x, got,
          halo, rims, part_src, part_tgt, part_mix, held_src, held_tgt, held_mix, *rest):
     send_sem, recv_sem, halo_send, halo_recv, rim_send, rim_recv, y_send, y_recv, load_sem = rest[-9:]
     bufs = rest[:-9]
@@ -255,14 +255,10 @@
     loads[1].wait()
     columns(own_src)
 
-    def turn_grid(m, _):
-        grid_x[:, pl.ds(pl.multiple_of(m * rows, rows), rows)] = grid[m].T
-        return 0
-
-    lax.fori_loop(0, members, turn_grid, 0)
     loads[2].wait()
 
-    gb = 32
+    gb = 16
+    chunks = rows // gb
 
     def forward(m, _):
         for one in halo_copies(m):
@@ -272,9 +268,9 @@
         proj[m, HALO + rows:ext] = edge[HALO:2 * HALO]
 
         linear = dot(hits[...], proj[m]) + count * tgt[m].astype(F32)
-        for at in range(0, rows, gb):
-            got = dot(pick[:, at:at + gb, :].reshape(nbrs * gb, ext), proj[m]).astype(BF)
-            got = got.reshape(nbrs, gb, width)
+
+        def edges(i):
+            at = i * gb
             for c in range(0, width, 256):
                 cols = slice(c, c + 256)
                 base = tgt[m, at:at + gb, cols]
@@ -282,7 +278,7 @@
                 acc_s = None
                 for k in range(nbrs):
                     on = maskb[k, at:at + gb, :]
-                    u = got[k, :, cols] + jnp.concatenate([on, on], axis=1) * base
+                    u = got[i % 2, k * gb:(k + 1) * gb, cols] + jnp.concatenate([on, on], axis=1) * base
                     t = jnp.tanh(u)
                     p = u * t
                     s = (t + u) - t * p
@@ -292,6 +288,17 @@
                 total = linear[at:at + gb, cols] + acc.astype(F32)
                 agg[m, at:at + gb, cols] = (0.25 * total).astype(BF)
                 slope_sum[m, at:at + gb, cols] = (acc_s.astype(F32) + count[at:at + gb]).astype(BF)
+
+        for i in range(chunks + 1):
+            if i < chunks:
+                rows_i = pick[:, i * gb:(i + 1) * gb, :].reshape(nbrs * gb, ext)
+                got[i % 2] = dot(rows_i, proj[m]).astype(BF)
+            if i == 0:
+                grid_x[:, pl.ds(pl.multiple_of(m * rows, rows), rows)] = grid[m].T
+                around = jnp.concatenate([halo[m, 0:HALO], lat[m], halo[m, HALO:2 * HALO]], axis=0)
+                lat_x[:, pl.ds(pl.multiple_of(m * ext, ext), ext)] = around.T
+            else:
+                edges(i - 1)
 
         h = grid[m].astype(F32) + dot(agg[m], wmix[...])
         mean = jnp.sum(h, axis=1, keepdims=True) * (1.0 / width)
@@ -310,8 +317,6 @@
         at = pl.ds(pl.multiple_of(m * rows, rows), rows)
         agg_x[:, at] = agg[m].T
         normed_x[:, at] = normed[m].T
-        around = jnp.concatenate([halo[m, 0:HALO], lat[m], halo[m, HALO:2 * HALO]], axis=0)
-        lat_x[:, pl.ds(pl.multiple_of(m * ext, ext), ext)] = around.T
         return 0
 
     lax.fori_loop(0, members, turn, 0)
@@ -384,19 +389,25 @@
     mix_l.s1()
     mix_r.s1()
 
+    def weigh(m, c):
+        cols = slice(c * CW, (c + 1) * CW)
+        for k in range(nbrs):
+            slope[m, k, :, cols] = slope[m, k, :, cols] * tgt[m, :, cols]
+
     def spread(m):
-        def column(cols):
-            d = tgt[m, :, cols]
-            for k in range(nbrs):
-                slope[m, k, :, cols] = slope[m, k, :, cols] * d
+        for c in range(tiles):
+            cols = slice(c * CW, (c + 1) * CW)
             edges = slope[m, :, :, cols].reshape(nbrs * rows, CW)
-            got = dot(pick_t[...], edges) + dot(hits_t[...], d)
-            dpe[m, :, cols] = got.astype(BF)
-
-        columns(column)
+            got_c = dot(pick_t[...], edges) + dot(hits_t[...], tgt[m, :, cols])
+            dpe[m, :, cols] = got_c.astype(BF)
+            if c + 1 < tiles:
+                weigh(m, c + 1)
+            elif m + 1 < members:
+                weigh(m + 1, 0)
         for one in rim_copies(m):
             one.start()
 
+    weigh(0, 0)
     spread(0)
     tgt_l.s1()
     tgt_r.s1()
@@ -540,6 +551,7 @@
             pltpu.VMEM((width, members * rows), BF),
             pltpu.VMEM((width, members * rows), BF),
             pltpu.VMEM((width, members * ext), BF),
+            pltpu.VMEM((2, nbrs * 16, width), BF),
             pltpu.VMEM((members, 2 * HALO, width), BF),
             pltpu.VMEM((members, 2 * HALO, width), BF),
             pltpu.VMEM((NC, NY, NX, NZ, 16, width), BF),

time: 85.2 us -> 85.5 us (level)
  no operation moved by 1% of the time
where the time goes in v4:
time: 85.5 us; the launch traced here: 84.1 us
  Pallas kernels  83.3 us (97%)
    pallas_call x1, Pallas kernels, on_device(): pl.pallas_call(body_, out_shape=[sds((members, rows, width), BF), sds((me...  80.4 us
    pallas_call x1, Pallas kernels, hand_over(): pl.pallas_call(move, out_shape=[jax.ShapeDtypeStruct(a.shape, a.dtype) fo...  2.99 us

profile of v4, /device:TPU:0, one launch (start us, length us, event | category | flops | bytes accessed | tf_op | source)
XLA Modules:
  0.0 84.1 jit_solution(7879941283136775725)
XLA Ops:
  0.6 80.4 %shard_map.145 = (bf16[4,128,1024]{2,1,0:T(8,128)(2,1)}, bf16[4,128,1024]{2,1,0:T(8,128)(2,1)}, f32[16,1024]{1,0:T(8,128)}, f32[16,1024]{1,0:T(8,128)}, f32[16,1024]{1,0:T(8,128)}, /*index=5*/f32[16,100]{1,0:T(8,128)}) custom-call(bf16[4,128,1024]{2,1,0:T(8,128)(2,1)} %refs_0_.1, bf16[4,128,1024]{2,1,0:T(8,128)(2,1)} %refs_1_.1, bf16[1024,1024]{1,0:T(8,128)(2,1)} %refs_2_.1, ...), custom_call_target="tpu_custom_call" | custom-call | flops 40000000000 | bytes 30000000 | tf_op jit(solution)/shard_map/pallas_call | solution.py:514
  81.0 3.0 %shard_map.146 = (bf16[4,128,1024]{2,1,0:T(8,128)(2,1)}, bf16[4,128,1024]{2,1,0:T(8,128)(2,1)}, f32[16,1024]{1,0:T(8,128)}, f32[16,1024]{1,0:T(8,128)}, f32[16,1024]{1,0:T(8,128)}, /*index=5*/f32[16,100]{1,0:T(8,128)}) custom-call(bf16[4,128,1024]{2,1,0:T(8,128)(2,1)} %get-tuple-element.12.refs_0_, bf16[4,128,1024]{2,1,0:T(8,128)(2,1)} %get-tuple-element.13.refs_1_, ...), custom_call_target="tpu_custom_call" | custom-call | tf_op jit(solution)/shard_map/pallas_call | solution.py:483

commit v5 on v3

--- a/solution.py
+++ b/solution.py
@@ -17,6 +17,9 @@
 CW = 512
 NY, NX, NZ, NC = 4, 4, 2, 2
 FP = 128
+MIX_CUTS = ((0, 512), (512, 512 + FP))
+TGT_CUTS = ((0, 512), (512, 512))
+SRC_CUTS = ((0, 256), (256, 256), (512, 256), (768, 256))
 
 
 def dot(a, b):
@@ -151,9 +154,9 @@
         part[b % 2, b // 16, (b // 4) % 4, (b // 2) % 2, :, cols] = block[b * 16:(b + 1) * 16]
 
 
-def body(scale, lat, grid, wsrc_in, wtgt_in, wmix_in, wout_in, truth_in, area_in, nbr, mask,
-         d_latent, d_grid, o_src, o_tgt, o_mix, o_out,
-         wsrc, wtgt, wmix, wout, truth, area,
+def body(scale, lat_in, grid_in, wsrc_in, wtgt_in, wmix_in, wout_in, truth_in, area_in, nbr, mask,
+         d_latent_out, d_grid_out, o_src, o_tgt, o_mix, o_out,
+         lat, grid, d_latent, d_grid, wsrc, wtgt, wmix, wout, truth, area,
          pick, pick_t, hits, hits_t, maskb, proj, tgt, slope, slope_sum, agg, normed, inv, ys, dys, dh, dq, dpe,
          agg_x, normed_x, grid_x, lat_x,
          halo, rims, part_src, part_tgt, part_mix, held_src, held_tgt, held_mix, *rest):
@@ -172,29 +175,28 @@
     for partner in place.partners:
         pl.semaphore_signal(barrier, inc=1, device_id=partner, device_id_type=MESH)
     loads = [pltpu.make_async_copy(src, dst, load_sem.at[i])
-             for i, (src, dst) in enumerate(((wtgt_in, wtgt), (wsrc_in, wsrc), (wmix_in, wmix)))]
+             for i, (src, dst) in enumerate(((lat_in, lat), (grid_in, grid), (wtgt_in, wtgt), (wsrc_in, wsrc),
+                                             (wmix_in, wmix)))]
     for one in loads:
         one.start()
 
-    def copies(src_up, src_down, dst, sems, m):
+    def copies(src, low, high, dst, sems, at, cols):
         return (
             pltpu.make_async_remote_copy(
-                src_ref=src_up, dst_ref=dst.at[m, pl.ds(0, HALO)],
-                send_sem=sems[0].at[0, m], recv_sem=sems[1].at[0, m],
+                src_ref=src.at[at[0], pl.ds(high, HALO), cols], dst_ref=dst.at[at[0], pl.ds(0, HALO), cols],
+                send_sem=sems[0].at[0, *at], recv_sem=sems[1].at[0, *at],
                 device_id=place.up, device_id_type=MESH),
             pltpu.make_async_remote_copy(
-                src_ref=src_down, dst_ref=dst.at[m, pl.ds(HALO, HALO)],
-                send_sem=sems[0].at[1, m], recv_sem=sems[1].at[1, m],
+                src_ref=src.at[at[0], pl.ds(low, HALO), cols], dst_ref=dst.at[at[0], pl.ds(HALO, HALO), cols],
+                send_sem=sems[0].at[1, *at], recv_sem=sems[1].at[1, *at],
                 device_id=place.down, device_id_type=MESH),
         )
 
     def halo_copies(m):
-        return copies(lat.at[m, pl.ds(rows - HALO, HALO)], lat.at[m, pl.ds(0, HALO)], halo,
-                      (halo_send, halo_recv), m)
-
-    def rim_copies(m):
-        return copies(dpe.at[m, pl.ds(HALO + rows, HALO)], dpe.at[m, pl.ds(0, HALO)], rims,
-                      (rim_send, rim_recv), m)
+        return copies(lat, 0, rows - HALO, halo, (halo_send, halo_recv), (m,), slice(None))
+
+    def rim_copies(m, c):
+        return copies(dpe, 0, HALO + rows, rims, (rim_send, rim_recv), (m, c), pl.ds(c * CW, CW))
 
     def y_copy(m):
         return pltpu.make_async_remote_copy(
@@ -202,6 +204,7 @@
             send_sem=y_send.at[m], recv_sem=y_recv.at[m],
             device_id=place.mate, device_id_type=MESH)
 
+    loads[0].wait()
     pl.semaphore_wait(barrier, len(place.partners))
     for m in range(members):
         for one in halo_copies(m):
@@ -250,9 +253,10 @@
         got = (0.5 * dot(lat[...].reshape(flat, width), wsrc[:, cols]).astype(BF)).astype(BF)
         proj[:, HALO:HALO + rows, cols] = got.reshape(members, rows, CW)
 
-    loads[0].wait()
+    loads[1].wait()
+    loads[2].wait()
     columns(own_tgt)
-    loads[1].wait()
+    loads[3].wait()
     columns(own_src)
 
     def turn_grid(m, _):
@@ -260,7 +264,7 @@
         return 0
 
     lax.fori_loop(0, members, turn_grid, 0)
-    loads[2].wait()
+    loads[4].wait()
 
     gb = 32
 
@@ -344,15 +348,18 @@
     lax.fori_loop(0, members, head, 0)
 
     halves = []
-    left = pl.ds(0, 512)
     at = 0
-    for part, held in ((part_mix, held_mix), (part_tgt, held_tgt), (part_src, held_src)):
-        wide = part.shape[-1]
-        halves.append(Half(place, wire, part, held, left, True, bufs[at:at + 2], bufs[at + 2]))
-        halves.append(Half(place, wire, part, held, pl.ds(512, wide - 512), False,
-                           bufs[at + 3:at + 5], bufs[at + 5]))
-        at += 6
-    mix_l, mix_r, tgt_l, tgt_r, src_l, src_r = halves
+    for part, held, cuts in ((part_mix, held_mix, MIX_CUTS), (part_tgt, held_tgt, TGT_CUTS),
+                             (part_src, held_src, SRC_CUTS)):
+        for i, (first, size) in enumerate(cuts):
+            halves.append(Half(place, wire, part, held, pl.ds(first, size), i % 2 == 0,
+                               bufs[at:at + 2], bufs[at + 2]))
+            at += 3
+    mix, tgt_sum, src = halves[:2], halves[2:4], halves[4:]
+
+    def each(parts, step):
+        for one in parts:
+            getattr(one, step)()
 
     def product(turned, right):
         return dot(turned[...], right.reshape(-1, right.shape[-1])).astype(BF)
@@ -361,10 +368,10 @@
         put(part_mix, product(agg_x, dh[:, :, cols]), cols)
 
     columns(mix_grad, 0, 1)
-    mix_l.start()
+    mix[0].start()
     columns(mix_grad, 1, 2)
     put(part_mix, product(normed_x, dys[...]), pl.ds(width, FP))
-    mix_r.start()
+    mix[1].start()
 
     def mix_back(cols):
         dagg = (0.125 * dot_nt(dh[...].reshape(flat, width), wmix[cols, :])).astype(BF)
@@ -378,64 +385,62 @@
         put(part_tgt, product(grid_x, dq[:, :, cols]), cols)
 
     columns(tgt_grad, 0, 1)
-    tgt_l.start()
+    tgt_sum[0].start()
     columns(tgt_grad, 1, 2)
-    tgt_r.start()
-    mix_l.s1()
-    mix_r.s1()
-
-    def spread(m):
-        def column(cols):
+    tgt_sum[1].start()
+    each(mix, "s1")
+
+    def spread(c, first, last):
+        cols = pl.ds(c * CW, CW)
+
+        def member(m, _):
             d = tgt[m, :, cols]
             for k in range(nbrs):
                 slope[m, k, :, cols] = slope[m, k, :, cols] * d
             edges = slope[m, :, :, cols].reshape(nbrs * rows, CW)
-            got = dot(pick_t[...], edges) + dot(hits_t[...], d)
-            dpe[m, :, cols] = got.astype(BF)
-
-        columns(column)
-        for one in rim_copies(m):
-            one.start()
-
-    spread(0)
-    tgt_l.s1()
-    tgt_r.s1()
-    spread(1)
-    spread(2)
-    mix_l.s2()
-    mix_r.s2()
-    spread(3)
+            dpe[m, :, cols] = (dot(pick_t[...], edges) + dot(hits_t[...], d)).astype(BF)
+            for one in rim_copies(m, c):
+                one.start()
+            return 0
+
+        lax.fori_loop(first, last, member, 0)
 
     def src_grad(cols):
         put(part_src, product(lat_x, dpe[:, :, cols]), cols)
-
-    columns(src_grad, 0, 1)
-    src_l.start()
-    tgt_l.s2()
-    tgt_r.s2()
-    columns(src_grad, 1, 2)
-    src_r.start()
-    mix_l.s3()
-    mix_r.s3()
-    src_l.s1()
 
     def grid_back(cols):
         got = dot_nt(dq[...].reshape(flat, width), wtgt[cols, :]).reshape(members, rows, CW)
         d_grid[:, :, cols] = (dh[:, :, cols].astype(F32) + got).astype(BF)
 
+    spread(0, 0, 2)
+    each(tgt_sum, "s1")
+    spread(0, 2, 4)
+    each(mix, "s2")
+    columns(src_grad, 0, 1)
+    each(src[:2], "start")
+    spread(1, 0, 2)
+    each(tgt_sum, "s2")
+    each(src[:2], "s1")
+    spread(1, 2, 4)
+    each(mix, "s3")
+    columns(src_grad, 1, 2)
+    each(src[2:], "start")
+    each(tgt_sum, "s3")
     columns(grid_back, 0, 1)
-    src_r.s1()
+    each(src[2:], "s1")
+    each(src[:2], "s2")
     columns(grid_back, 1, 2)
-    tgt_l.s3()
-    tgt_r.s3()
-    o_mix[:, 0:512] = mix_l.s4(scale)
-    last = mix_r.s4(scale)
+    out_grid = pltpu.make_async_copy(d_grid, d_grid_out, load_sem.at[5])
+    out_grid.start()
+    o_mix[:, 0:512] = mix[0].s4(scale)
+    last = mix[1].s4(scale)
     o_mix[:, 512:width] = last[:, 0:width - 512]
     o_out[...] = last[:, width - 512:width - 512 + fields]
 
     def sum_rims(m, _):
-        for one in rim_copies(m):
-            one.wait()
+        for c in range(tiles):
+            for one in rim_copies(m, c):
+                one.wait()
         dq[m] = (dpe[m, HALO:HALO + rows].astype(F32) + rims[m].astype(F32)).astype(BF)
         return 0
 
@@ -446,15 +451,18 @@
         d_latent[:, :, cols] = got.astype(BF)
 
     columns(latent_back, 0, 1)
-    src_l.s2()
+    each(src[:2], "s3")
     columns(latent_back, 1, 2)
-    src_r.s2()
-    src_l.s3()
-    src_r.s3()
-    o_tgt[:, 0:512] = tgt_l.s4(scale)
-    o_tgt[:, 512:width] = tgt_r.s4(scale)
-    o_src[:, 0:512] = src_l.s4(scale)
-    o_src[:, 512:width] = src_r.s4(scale)
+    out_latent = pltpu.make_async_copy(d_latent, d_latent_out, load_sem.at[6])
+    out_latent.start()
+    each(src[2:], "s2")
+    for one, (first, size) in zip(tgt_sum, TGT_CUTS):
+        o_tgt[:, first:first + size] = one.s4(scale)
+    each(src[2:], "s3")
+    out_grid.wait()
+    out_latent.wait()
+    for one, (first, size) in zip(src, SRC_CUTS):
+        o_src[:, first:first + size] = one.s4(scale)
 
 
 def hand_over(arrays):
@@ -498,7 +506,7 @@
     hbm = pl.BlockSpec(memory_space=pl.ANY)
     sds = jax.ShapeDtypeStruct
     wide = width + FP
-    halves = (512, wide - 512, 512, width - 512, 512, width - 512)
+    halves = [size for cuts in (MIX_CUTS, TGT_CUTS, SRC_CUTS) for _, size in cuts]
     ncopies = 10 * len(halves)
     results = pl.pallas_call(
         body_,
@@ -510,9 +518,13 @@
             sds((16, width), F32),
             sds((16, fields), F32),
         ],
-        in_specs=[vm, vm, hbm, hbm, hbm, vm, vm, vm, vm, vm],
-        out_specs=[vm] * 6,
+        in_specs=[hbm, hbm, hbm, hbm, hbm, vm, vm, vm, vm, vm],
+        out_specs=[hbm, hbm, vm, vm, vm, vm],
         scratch_shapes=[
+            pltpu.VMEM((members, rows, width), BF),
+            pltpu.VMEM((members, rows, width), BF),
+            pltpu.VMEM((members, rows, width), BF),
+            pltpu.VMEM((members, rows, width), BF),
             pltpu.VMEM((width, width), BF),
             pltpu.VMEM((width, width), BF),
             pltpu.VMEM((width, width), BF),
@@ -553,11 +565,11 @@
             pltpu.SemaphoreType.DMA((ncopies,)),
             pltpu.SemaphoreType.DMA((2, members)),
             pltpu.SemaphoreType.DMA((2, members)),
-            pltpu.SemaphoreType.DMA((2, members)),
-            pltpu.SemaphoreType.DMA((2, members)),
+            pltpu.SemaphoreType.DMA((2, members, width // CW)),
+            pltpu.SemaphoreType.DMA((2, members, width // CW)),
             pltpu.SemaphoreType.DMA((members,)),
             pltpu.SemaphoreType.DMA((members,)),
-            pltpu.SemaphoreType.DMA((3,)),
+            pltpu.SemaphoreType.DMA((8,)),
         ],
         compiler_params=pltpu.CompilerParams(
             collective_id=0, has_side_effects=True, vmem_limit_bytes=63 * 2**20

time: 85.2 us -> 85.4 us (level); the launches traced: 83.8 us -> 85.2 us
  Pallas kernels: 83 us -> 84.4 us
    pallas_call x1, Pallas kernels: 80 us -> 81.4 us  [on_device(): pl.pallas_call(body_, out_shape=[sds((members, rows, width), BF), sds((me...]
where the time goes in v5:
time: 85.4 us; the launch traced here: 85.2 us
  Pallas kernels  84.4 us (99%)
    pallas_call x1, Pallas kernels, on_device(): pl.pallas_call(body_, out_shape=[sds((members, rows, width), BF), sds((me...  81.4 us
    pallas_call x1, Pallas kernels, hand_over(): pl.pallas_call(move, out_shape=[jax.ShapeDtypeStruct(a.shape, a.dtype) fo...  2.99 us

profile of v5, /device:TPU:0, one launch (start us, length us, event | category | flops | bytes accessed | tf_op | source)
XLA Modules:
  0.0 85.2 jit_solution(2601364884929988331)
XLA Ops:
  0.6 81.4 %shard_map.145 = (bf16[4,128,1024]{2,1,0:T(8,128)(2,1)}, bf16[4,128,1024]{2,1,0:T(8,128)(2,1)}, f32[16,1024]{1,0:T(8,128)}, f32[16,1024]{1,0:T(8,128)}, f32[16,1024]{1,0:T(8,128)}, /*index=5*/f32[16,100]{1,0:T(8,128)}) custom-call(bf16[4,128,1024]{2,1,0:T(8,128)(2,1)} %refs_0_.1, bf16[4,128,1024]{2,1,0:T(8,128)(2,1)} %refs_1_.1, bf16[1024,1024]{1,0:T(8,128)(2,1)} %refs_2_.1, ...), custom_call_target="tpu_custom_call" | custom-call | flops 40000000000 | bytes 30000000 | tf_op jit(solution)/shard_map/pallas_call | solution.py:511
  82.1 3.0 %shard_map.146 = (bf16[4,128,1024]{2,1,0:T(8,128)(2,1)}, bf16[4,128,1024]{2,1,0:T(8,128)(2,1)}, f32[16,1024]{1,0:T(8,128)}, f32[16,1024]{1,0:T(8,128)}, f32[16,1024]{1,0:T(8,128)}, /*index=5*/f32[16,100]{1,0:T(8,128)}) custom-call(bf16[4,128,1024]{2,1,0:T(8,128)(2,1)} %get-tuple-element.12.refs_0_, bf16[4,128,1024]{2,1,0:T(8,128)(2,1)} %get-tuple-element.13.refs_1_, ...), custom_call_target="tpu_custom_call" | custom-call | tf_op jit(solution)/shard_map/pallas_call | solution.py:480

commit v6 on v5

--- a/solution.py
+++ b/solution.py
@@ -95,31 +95,27 @@
 
 
 class Half:
-    def __init__(self, place, wire, part, held, cols, y_first, bufs, zbuf):
-        self.place, self.wire, self.zbuf, self.cols = place, wire, zbuf, cols
+    def __init__(self, place, wire, y_first, part, held, wide, thin, zbuf):
+        self.place, self.wire, self.zbuf = place, wire, zbuf
         self.part, self.held = part, held
         y, x = place.y, place.x
-
         on_y, on_x = (y, place.y_ring), (x, place.x_ring)
         if y_first:
-            self.one = Swap(wire, *on_y, lambda d: held.at[d, :, :, :, cols], bufs[0])
-            self.two = Swap(wire, *on_x, lambda d: held.at[y, d, :, :, cols], bufs[1])
+            self.one = Swap(wire, *on_y, lambda d: held.at[d], wide)
+            self.two = Swap(wire, *on_x, lambda d: held.at[y, d], thin)
         else:
-            self.one = Swap(wire, *on_x, lambda d: held.at[:, d, :, :, cols], bufs[0])
-            self.two = Swap(wire, *on_y, lambda d: held.at[d, x, :, :, cols], bufs[1])
+            self.one = Swap(wire, *on_x, lambda d: held.at[:, d], wide)
+            self.two = Swap(wire, *on_y, lambda d: held.at[d, x], thin)
 
     def start(self):
-        cols = self.cols
-        self.cross = self.wire.copy(self.part.at[1 - self.place.c, :, :, :, :, cols],
-                                    self.held.at[:, :, :, :, cols], self.place.core)
+        self.cross = self.wire.copy(self.part.at[1 - self.place.c], self.held, self.place.core)
         self.cross.start()
 
     def s1(self):
         self.cross.wait()
-        cols = self.cols
 
         def add(yy, _):
-            add_into(self.held.at[yy, :, :, :, cols], self.part.at[self.place.c, yy, :, :, :, cols])
+            add_into(self.held.at[yy], self.part.at[self.place.c, yy])
             return 0
 
         lax.fori_loop(0, NY, add, 0)
@@ -133,9 +129,9 @@
         self.two.finish()
         p = self.place
         mine = self.held.at[p.y, p.x]
-        self.last = [self.wire.copy(mine.at[p.z, :, self.cols], self.zbuf.at[0], p.mate),
-                     self.wire.copy(mine.at[1 - p.z, :, self.cols], self.zbuf.at[1], p.z_far),
-                     self.wire.copy(mine.at[1 - p.z, :, self.cols], self.zbuf.at[2], p.z_both)]
+        self.last = [self.wire.copy(mine.at[p.z], self.zbuf.at[0], p.mate),
+                     self.wire.copy(mine.at[1 - p.z], self.zbuf.at[1], p.z_far),
+                     self.wire.copy(mine.at[1 - p.z], self.zbuf.at[2], p.z_both)]
         for one in self.last:
             one.start()
 
@@ -143,13 +139,14 @@
         p = self.place
         for one in self.last:
             one.wait()
-        total = self.held[p.y, p.x, p.z, :, self.cols].astype(F32)
+        total = self.held[p.y, p.x, p.z].astype(F32)
         for k in range(3):
             total = total + self.zbuf[k].astype(F32)
         return total * scale
 
 
-def put(part, block, cols):
+def put(part, block, first=0):
+    cols = slice(first, first + block.shape[1])
     for b in range(NY * NX * NZ * NC):
         part[b % 2, b // 16, (b // 4) % 4, (b // 2) % 2, :, cols] = block[b * 16:(b + 1) * 16]
 
@@ -159,7 +156,7 @@
          lat, grid, d_latent, d_grid, wsrc, wtgt, wmix, wout, truth, area,
          pick, pick_t, hits, hits_t, maskb, proj, tgt, slope, slope_sum, agg, normed, inv, ys, dys, dh, dq, dpe,
          agg_x, normed_x, grid_x, lat_x,
-         halo, rims, part_src, part_tgt, part_mix, held_src, held_tgt, held_mix, *rest):
+         halo, rims, *rest):
     send_sem, recv_sem, halo_send, halo_recv, rim_send, rim_recv, y_send, y_recv, load_sem = rest[-9:]
     bufs = rest[:-9]
     members, rows, width = grid.shape
@@ -347,14 +344,7 @@
 
     lax.fori_loop(0, members, head, 0)
 
-    halves = []
-    at = 0
-    for part, held, cuts in ((part_mix, held_mix, MIX_CUTS), (part_tgt, held_tgt, TGT_CUTS),
-                             (part_src, held_src, SRC_CUTS)):
-        for i, (first, size) in enumerate(cuts):
-            halves.append(Half(place, wire, part, held, pl.ds(first, size), i % 2 == 0,
-                               bufs[at:at + 2], bufs[at + 2]))
-            at += 3
+    halves = [Half(place, wire, i % 2 == 0, *bufs[5 * i:5 * i + 5]) for i in range(len(bufs) // 5)]
     mix, tgt_sum, src = halves[:2], halves[2:4], halves[4:]
 
     def each(parts, step):
@@ -365,12 +355,12 @@
         return dot(turned[...], right.reshape(-1, right.shape[-1])).astype(BF)
 
     def mix_grad(cols):
-        put(part_mix, product(agg_x, dh[:, :, cols]), cols)
-
-    columns(mix_grad, 0, 1)
+        return product(agg_x, dh[:, :, cols])
+
+    put(mix[0].part, mix_grad(pl.ds(0, CW)))
     mix[0].start()
-    columns(mix_grad, 1, 2)
-    put(part_mix, product(normed_x, dys[...]), pl.ds(width, FP))
+    put(mix[1].part, mix_grad(pl.ds(CW, CW)))
+    put(mix[1].part, product(normed_x, dys[...]), CW)
     mix[1].start()
 
     def mix_back(cols):
@@ -382,11 +372,11 @@
     columns(mix_back)
 
     def tgt_grad(cols):
-        put(part_tgt, product(grid_x, dq[:, :, cols]), cols)
-
-    columns(tgt_grad, 0, 1)
+        return product(grid_x, dq[:, :, cols])
+
+    put(tgt_sum[0].part, tgt_grad(pl.ds(0, CW)))
     tgt_sum[0].start()
-    columns(tgt_grad, 1, 2)
+    put(tgt_sum[1].part, tgt_grad(pl.ds(CW, CW)))
     tgt_sum[1].start()
     each(mix, "s1")
 
@@ -405,8 +395,10 @@
 
         lax.fori_loop(first, last, member, 0)
 
-    def src_grad(cols):
-        put(part_src, product(lat_x, dpe[:, :, cols]), cols)
+    def src_grad(c):
+        block = product(lat_x, dpe[:, :, c * CW:(c + 1) * CW])
+        for i in range(2):
+            put(src[2 * c + i].part, block[:, i * 256:(i + 1) * 256])
 
     def grid_back(cols):
         got = dot_nt(dq[...].reshape(flat, width), wtgt[cols, :]).reshape(members, rows, CW)
@@ -416,14 +408,14 @@
     each(tgt_sum, "s1")
     spread(0, 2, 4)
     each(mix, "s2")
-    columns(src_grad, 0, 1)
+    src_grad(0)
     each(src[:2], "start")
     spread(1, 0, 2)
     each(tgt_sum, "s2")
     each(src[:2], "s1")
     spread(1, 2, 4)
     each(mix, "s3")
-    columns(src_grad, 1, 2)
+    src_grad(1)
     each(src[2:], "start")
     each(tgt_sum, "s3")
     columns(grid_back, 0, 1)
@@ -499,13 +491,13 @@
         body(scale, *refs)
 
     def ring_bufs(cols):
-        return [pltpu.VMEM((3, 4, 2, 16, cols), BF), pltpu.VMEM((3, 2, 16, cols), BF),
+        return [pltpu.VMEM((NC, NY, NX, NZ, 16, cols), BF), pltpu.VMEM((NY, NX, NZ, 16, cols), BF),
+                pltpu.VMEM((3, 4, NZ, 16, cols), BF), pltpu.VMEM((3, NZ, 16, cols), BF),
                 pltpu.VMEM((3, 16, cols), BF)]
 
     vm = pl.BlockSpec(memory_space=pltpu.VMEM)
     hbm = pl.BlockSpec(memory_space=pl.ANY)
     sds = jax.ShapeDtypeStruct
-    wide = width + FP
     halves = [size for cuts in (MIX_CUTS, TGT_CUTS, SRC_CUTS) for _, size in cuts]
     ncopies = 10 * len(halves)
     results = pl.pallas_call(
@@ -554,12 +546,6 @@
             pltpu.VMEM((width, members * ext), BF),
             pltpu.VMEM((members, 2 * HALO, width), BF),
             pltpu.VMEM((members, 2 * HALO, width), BF),
-            pltpu.VMEM((NC, NY, NX, NZ, 16, width), BF),
-            pltpu.VMEM((NC, NY, NX, NZ, 16, width), BF),
-            pltpu.VMEM((NC, NY, NX, NZ, 16, wide), BF),
-            pltpu.VMEM((NY, NX, NZ, 16, width), BF),
-            pltpu.VMEM((NY, NX, NZ, 16, width), BF),
-            pltpu.VMEM((NY, NX, NZ, 16, wide), BF),
             *[buf for cols in halves for buf in ring_bufs(cols)],
             pltpu.SemaphoreType.DMA((ncopies,)),
             pltpu.SemaphoreType.DMA((ncopies,)),

time: 85.4 us -> 85.4 us (level)
  no operation moved by 1% of the time
where the time goes in v6:
time: 85.4 us; the launch traced here: 85.3 us
  Pallas kernels  84.4 us (99%)
    pallas_call x1, Pallas kernels, on_device(): pl.pallas_call(body_, out_shape=[sds((members, rows, width), BF), sds((me...  81.5 us
    pallas_call x1, Pallas kernels, hand_over(): pl.pallas_call(move, out_shape=[jax.ShapeDtypeStruct(a.shape, a.dtype) fo...  2.99 us

profile of v6, /device:TPU:0, one launch (start us, length us, event | category | flops | bytes accessed | tf_op | source)
XLA Modules:
  0.0 85.3 jit_solution(3768027578575719203)
XLA Ops:
  0.6 81.5 %shard_map.145 = (bf16[4,128,1024]{2,1,0:T(8,128)(2,1)}, bf16[4,128,1024]{2,1,0:T(8,128)(2,1)}, f32[16,1024]{1,0:T(8,128)}, f32[16,1024]{1,0:T(8,128)}, f32[16,1024]{1,0:T(8,128)}, /*index=5*/f32[16,100]{1,0:T(8,128)}) custom-call(bf16[4,128,1024]{2,1,0:T(8,128)(2,1)} %refs_0_.1, bf16[4,128,1024]{2,1,0:T(8,128)(2,1)} %refs_1_.1, bf16[1024,1024]{1,0:T(8,128)(2,1)} %refs_2_.1, ...), custom_call_target="tpu_custom_call" | custom-call | flops 40000000000 | bytes 30000000 | tf_op jit(solution)/shard_map/pallas_call | solution.py:503
  82.1 3.0 %shard_map.146 = (bf16[4,128,1024]{2,1,0:T(8,128)(2,1)}, bf16[4,128,1024]{2,1,0:T(8,128)(2,1)}, f32[16,1024]{1,0:T(8,128)}, f32[16,1024]{1,0:T(8,128)}, f32[16,1024]{1,0:T(8,128)}, /*index=5*/f32[16,100]{1,0:T(8,128)}) custom-call(bf16[4,128,1024]{2,1,0:T(8,128)(2,1)} %get-tuple-element.12.refs_0_, bf16[4,128,1024]{2,1,0:T(8,128)(2,1)} %get-tuple-element.13.refs_1_, ...), custom_call_target="tpu_custom_call" | custom-call | tf_op jit(solution)/shard_map/pallas_call | solution.py:472

commit v7 on v6

--- a/solution.py
+++ b/solution.py
@@ -19,7 +19,7 @@
 FP = 128
 MIX_CUTS = ((0, 512), (512, 512 + FP))
 TGT_CUTS = ((0, 512), (512, 512))
-SRC_CUTS = ((0, 256), (256, 256), (512, 256), (768, 256))
+SRC_CUTS = ((0, 512), (512, 512))
 
 
 def dot(a, b):
@@ -40,16 +40,20 @@
         t = lax.axis_index("grid")
         tiles = NY * NX * NZ * NC
         self.y, self.x, self.z, self.c = t // 16, (t // 4) % 4, (t // 2) % 2, t % 2
-        self.up = (self.me, (t + 1) % tiles)
-        self.down = (self.me, (t + tiles - 1) % tiles)
+        step = 2 * self.c - 1
+        far = (t + step + tiles) % tiles
+        turned = self.at(z=1 - self.z)[1]
+        self.by_mate = (1 - self.me, far)
+        self.by_both = (1 - self.me, (turned + step + tiles) % tiles)
+        from_both = (1 - self.me, far + 2 - 4 * ((far // 2) % 2))
         self.mate = (1 - self.me, t)
         self.core = self.at(c=1 - self.c)
         self.y_ring = tuple(self.at(y=(self.y + k) % 4) for k in (1, 2, 3))
         self.x_ring = tuple(self.at(x=(self.x + k) % 4) for k in (1, 2, 3))
         self.z_far = (self.me, self.at(z=1 - self.z)[1])
         self.z_both = (1 - self.me, self.z_far[1])
-        self.partners = (self.up, self.down, self.core, *self.y_ring, *self.x_ring,
-                         self.mate, self.z_far, self.z_both)
+        self.partners = (self.core, *self.y_ring, *self.x_ring, self.mate, self.z_far, self.z_both,
+                         self.by_mate, from_both)
 
     def at(self, y=None, x=None, z=None, c=None):
         y = self.y if y is None else y
@@ -153,10 +157,10 @@
 
 def body(scale, lat_in, grid_in, wsrc_in, wtgt_in, wmix_in, wout_in, truth_in, area_in, nbr, mask,
          d_latent_out, d_grid_out, o_src, o_tgt, o_mix, o_out,
-         lat, grid, d_latent, d_grid, wsrc, wtgt, wmix, wout, truth, area,
+         lat, grid, wsrc, wtgt, wmix, wout, truth, area,
          pick, pick_t, hits, hits_t, maskb, proj, tgt, slope, slope_sum, agg, normed, inv, ys, dys, dh, dq, dpe,
          agg_x, normed_x, grid_x, lat_x,
-         halo, rims, *rest):
+         halo, rims, halo_hop, rim_hop, *rest):
     send_sem, recv_sem, halo_send, halo_recv, rim_send, rim_recv, y_send, y_recv, load_sem = rest[-9:]
     bufs = rest[:-9]
     members, rows, width = grid.shape
@@ -165,6 +169,7 @@
     ext = rows + 2 * HALO
     tiles = width // CW
     flat = members * rows
+    d_latent, d_grid = agg, normed
     place = Place()
     wire = Wire(send_sem, recv_sem)
 
@@ -177,23 +182,49 @@
     for one in loads:
         one.start()
 
-    def copies(src, low, high, dst, sems, at, cols):
-        return (
-            pltpu.make_async_remote_copy(
-                src_ref=src.at[at[0], pl.ds(high, HALO), cols], dst_ref=dst.at[at[0], pl.ds(0, HALO), cols],
-                send_sem=sems[0].at[0, *at], recv_sem=sems[1].at[0, *at],
-                device_id=place.up, device_id_type=MESH),
-            pltpu.make_async_remote_copy(
-                src_ref=src.at[at[0], pl.ds(low, HALO), cols], dst_ref=dst.at[at[0], pl.ds(HALO, HALO), cols],
-                send_sem=sems[0].at[1, *at], recv_sem=sems[1].at[1, *at],
-                device_id=place.down, device_id_type=MESH),
-        )
-
-    def halo_copies(m):
-        return copies(lat, 0, rows - HALO, halo, (halo_send, halo_recv), (m,), slice(None))
-
-    def rim_copies(m, c):
-        return copies(dpe, 0, HALO + rows, rims, (rim_send, rim_recv), (m, c), pl.ds(c * CW, CW))
+    def remote(src, dst, send, recv, device):
+        return pltpu.make_async_remote_copy(src_ref=src, dst_ref=dst, send_sem=send, recv_sem=recv,
+                                            device_id=device, device_id_type=MESH)
+
+    class Edge:
+        def __init__(self, src, length, dst, hop, sems):
+            self.src, self.dst, self.hop = src, dst, hop
+            self.last = length - HALO
+            self.send, self.recv = sems
+
+        def near(self, m):
+            c = place.c
+            return remote(self.src.at[m, pl.ds((1 - c) * self.last, HALO)],
+                          self.dst.at[m, pl.ds(c * HALO, HALO)],
+                          self.send.at[0, m], self.recv.at[0, m], place.core)
+
+        def first(self, m, r):
+            part = pl.ds(place.c * self.last + r * (HALO // 2), HALO // 2)
+            return remote(self.src.at[m, part], self.hop.at[r, m], self.send.at[1 + r, m], self.recv.at[1 + r, m],
+                          (place.mate, place.z_both)[r])
+
+        def second(self, m, r):
+            part = pl.ds((1 - place.c) * HALO + r * (HALO // 2), HALO // 2)
+            return remote(self.hop.at[r, m], self.dst.at[m, part], self.send.at[3 + r, m], self.recv.at[3 + r, m],
+                          (place.by_mate, place.by_both)[r])
+
+        def start(self, m):
+            self.first(m, 0).start()
+            self.first(m, 1).start()
+            self.near(m).start()
+
+        def relay(self, m):
+            for r in range(2):
+                self.first(m, r).wait()
+                self.second(m, r).start()
+
+        def wait(self, m):
+            self.near(m).wait()
+            self.second(m, 0).wait()
+            self.second(m, 1).wait()
+
+    halo_rows = Edge(lat, rows, halo, halo_hop, (halo_send, halo_recv))
+    rim_rows = Edge(dpe, ext, rims, rim_hop, (rim_send, rim_recv))
 
     def y_copy(m):
         return pltpu.make_async_remote_copy(
@@ -204,8 +235,7 @@
     loads[0].wait()
     pl.semaphore_wait(barrier, len(place.partners))
     for m in range(members):
-        for one in halo_copies(m):
-            one.start()
+        halo_rows.start(m)
 
     truth[...] = jnp.zeros_like(truth)
     truth[0:fields, :] = truth_in[...]
@@ -250,24 +280,27 @@
         got = (0.5 * dot(lat[...].reshape(flat, width), wsrc[:, cols]).astype(BF)).astype(BF)
         proj[:, HALO:HALO + rows, cols] = got.reshape(members, rows, CW)
 
+    halo_rows.relay(0)
     loads[1].wait()
     loads[2].wait()
     columns(own_tgt)
+    halo_rows.relay(1)
     loads[3].wait()
     columns(own_src)
+    halo_rows.relay(2)
 
     def turn_grid(m, _):
         grid_x[:, pl.ds(pl.multiple_of(m * rows, rows), rows)] = grid[m].T
         return 0
 
     lax.fori_loop(0, members, turn_grid, 0)
+    halo_rows.relay(3)
     loads[4].wait()
 
     gb = 32
 
     def forward(m, _):
-        for one in halo_copies(m):
-            one.wait()
+        halo_rows.wait(m)
         edge = (0.5 * dot(halo[m], wsrc[...]).astype(BF)).astype(BF)
         proj[m, 0:HALO] = edge[0:HALO]
         proj[m, HALO + rows:ext] = edge[HALO:2 * HALO]
@@ -380,48 +413,45 @@
     tgt_sum[1].start()
     each(mix, "s1")
 
-    def spread(c, first, last):
-        cols = pl.ds(c * CW, CW)
-
-        def member(m, _):
+    def spread(m):
+        def column(cols):
             d = tgt[m, :, cols]
             for k in range(nbrs):
                 slope[m, k, :, cols] = slope[m, k, :, cols] * d
             edges = slope[m, :, :, cols].reshape(nbrs * rows, CW)
             dpe[m, :, cols] = (dot(pick_t[...], edges) + dot(hits_t[...], d)).astype(BF)
-            for one in rim_copies(m, c):
-                one.start()
-            return 0
-
-        lax.fori_loop(first, last, member, 0)
+
+        columns(column)
+        rim_rows.start(m)
 
     def src_grad(c):
-        block = product(lat_x, dpe[:, :, c * CW:(c + 1) * CW])
-        for i in range(2):
-            put(src[2 * c + i].part, block[:, i * 256:(i + 1) * 256])
+        put(src[c].part, product(lat_x, dpe[:, :, c * CW:(c + 1) * CW]))
 
     def grid_back(cols):
         got = dot_nt(dq[...].reshape(flat, width), wtgt[cols, :]).reshape(members, rows, CW)
         d_grid[:, :, cols] = (dh[:, :, cols].astype(F32) + got).astype(BF)
 
-    spread(0, 0, 2)
+    spread(0)
     each(tgt_sum, "s1")
-    spread(0, 2, 4)
+    spread(1)
+    rim_rows.relay(0)
+    spread(2)
+    rim_rows.relay(1)
     each(mix, "s2")
+    spread(3)
+    rim_rows.relay(2)
     src_grad(0)
-    each(src[:2], "start")
-    spread(1, 0, 2)
+    src[0].start()
+    rim_rows.relay(3)
     each(tgt_sum, "s2")
-    each(src[:2], "s1")
-    spread(1, 2, 4)
+    src_grad(1)
+    src[1].start()
     each(mix, "s3")
-    src_grad(1)
-    each(src[2:], "start")
+    src[0].s1()
+    columns(grid_back, 0, 1)
+    src[1].s1()
+    columns(grid_back, 1, 2)
     each(tgt_sum, "s3")
-    columns(grid_back, 0, 1)
-    each(src[2:], "s1")
-    each(src[:2], "s2")
-    columns(grid_back, 1, 2)
     out_grid = pltpu.make_async_copy(d_grid, d_grid_out, load_sem.at[5])
     out_grid.start()
     o_mix[:, 0:512] = mix[0].s4(scale)
@@ -430,9 +460,7 @@
     o_out[...] = last[:, width - 512:width - 512 + fields]
 
     def sum_rims(m, _):
-        for c in range(tiles):
-            for one in rim_copies(m, c):
-                one.wait()
+        rim_rows.wait(m)
         dq[m] = (dpe[m, HALO:HALO + rows].astype(F32) + rims[m].astype(F32)).astype(BF)
         return 0
 
@@ -443,14 +471,14 @@
         d_latent[:, :, cols] = got.astype(BF)
 
     columns(latent_back, 0, 1)
-    each(src[:2], "s3")
+    src[0].s2()
     columns(latent_back, 1, 2)
     out_latent = pltpu.make_async_copy(d_latent, d_latent_out, load_sem.at[6])
     out_latent.start()
-    each(src[2:], "s2")
+    src[1].s2()
     for one, (first, size) in zip(tgt_sum, TGT_CUTS):
         o_tgt[:, first:first + size] = one.s4(scale)
-    each(src[2:], "s3")
+    each(src, "s3")
     out_grid.wait()
     out_latent.wait()
     for one, (first, size) in zip(src, SRC_CUTS):
@@ -515,8 +543,6 @@
         scratch_shapes=[
             pltpu.VMEM((members, rows, width), BF),
             pltpu.VMEM((members, rows, width), BF),
-            pltpu.VMEM((members, rows, width), BF),
-            pltpu.VMEM((members, rows, width), BF),
             pltpu.VMEM((width, width), BF),
             pltpu.VMEM((width, width), BF),
             pltpu.VMEM((width, width), BF),
@@ -546,13 +572,15 @@
             pltpu.VMEM((width, members * ext), BF),
             pltpu.VMEM((members, 2 * HALO, width), BF),
             pltpu.VMEM((members, 2 * HALO, width), BF),
+            pltpu.VMEM((2, members, HALO // 2, width), BF),
+            pltpu.VMEM((2, members, HALO // 2, width), BF),
             *[buf for cols in halves for buf in ring_bufs(cols)],
             pltpu.SemaphoreType.DMA((ncopies,)),
             pltpu.SemaphoreType.DMA((ncopies,)),
-            pltpu.SemaphoreType.DMA((2, members)),
-            pltpu.SemaphoreType.DMA((2, members)),
-            pltpu.SemaphoreType.DMA((2, members, width // CW)),
-            pltpu.SemaphoreType.DMA((2, members, width // CW)),
+            pltpu.SemaphoreType.DMA((5, members)),
+            pltpu.SemaphoreType.DMA((5, members)),
+            pltpu.SemaphoreType.DMA((5, members)),
+            pltpu.SemaphoreType.DMA((5, members)),
             pltpu.SemaphoreType.DMA((members,)),
             pltpu.SemaphoreType.DMA((members,)),
             pltpu.SemaphoreType.DMA((8,)),

time: 85.4 us -> 85.7 us (level)
  no operation moved by 1% of the time
where the time goes in v7:
time: 85.7 us; the launch traced here: 85.5 us
  Pallas kernels  84.7 us (99%)
    pallas_call x1, Pallas kernels, on_device(): pl.pallas_call(body_, out_shape=[sds((members, rows, width), BF), sds((me...  81.7 us
    pallas_call x1, Pallas kernels, hand_over(): pl.pallas_call(move, out_shape=[jax.ShapeDtypeStruct(a.shape, a.dtype) fo...  2.99 us

profile of v7, /device:TPU:0, one launch (start us, length us, event | category | flops | bytes accessed | tf_op | source)
XLA Modules:
  0.0 85.5 jit_solution(9020861591786734806)
XLA Ops:
  0.6 81.7 %shard_map.145 = (bf16[4,128,1024]{2,1,0:T(8,128)(2,1)}, bf16[4,128,1024]{2,1,0:T(8,128)(2,1)}, f32[16,1024]{1,0:T(8,128)}, f32[16,1024]{1,0:T(8,128)}, f32[16,1024]{1,0:T(8,128)}, /*index=5*/f32[16,100]{1,0:T(8,128)}) custom-call(bf16[4,128,1024]{2,1,0:T(8,128)(2,1)} %refs_0_.1, bf16[4,128,1024]{2,1,0:T(8,128)(2,1)} %refs_1_.1, bf16[1024,1024]{1,0:T(8,128)(2,1)} %refs_2_.1, ...), custom_call_target="tpu_custom_call" | custom-call | flops 40000000000 | bytes 30000000 | tf_op jit(solution)/shard_map/pallas_call | solution.py:531
  82.4 3.0 %shard_map.146 = (bf16[4,128,1024]{2,1,0:T(8,128)(2,1)}, bf16[4,128,1024]{2,1,0:T(8,128)(2,1)}, f32[16,1024]{1,0:T(8,128)}, f32[16,1024]{1,0:T(8,128)}, f32[16,1024]{1,0:T(8,128)}, /*index=5*/f32[16,100]{1,0:T(8,128)}) custom-call(bf16[4,128,1024]{2,1,0:T(8,128)(2,1)} %get-tuple-element.12.refs_0_, bf16[4,128,1024]{2,1,0:T(8,128)(2,1)} %get-tuple-element.13.refs_1_, ...), custom_call_target="tpu_custom_call" | custom-call | tf_op jit(solution)/shard_map/pallas_call | solution.py:500

commit v8 on v6

--- a/solution.py
+++ b/solution.py
@@ -153,7 +153,7 @@
 
 def body(scale, lat_in, grid_in, wsrc_in, wtgt_in, wmix_in, wout_in, truth_in, area_in, nbr, mask,
          d_latent_out, d_grid_out, o_src, o_tgt, o_mix, o_out,
-         lat, grid, d_latent, d_grid, wsrc, wtgt, wmix, wout, truth, area,
+         lat, grid, wsrc, wtgt, wmix, wout, truth, area,
          pick, pick_t, hits, hits_t, maskb, proj, tgt, slope, slope_sum, agg, normed, inv, ys, dys, dh, dq, dpe,
          agg_x, normed_x, grid_x, lat_x,
          halo, rims, *rest):
@@ -165,6 +165,7 @@
     ext = rows + 2 * HALO
     tiles = width // CW
     flat = members * rows
+    d_latent, d_grid = agg, normed
     place = Place()
     wire = Wire(send_sem, recv_sem)
 
@@ -225,7 +226,7 @@
         one = (col == lane).astype(F32).astype(BF)
         one_t = (code[k:k + 1, :] == sub).astype(F32).astype(BF)
         pick[k] = one
-        maskb[k] = jnp.broadcast_to(on, (rows, 128)).astype(BF)
+        maskb[k] = jnp.broadcast_to(on, (rows, 128))
         count = count + on
         pick_t[:, k * rows:(k + 1) * rows] = one_t
         if k == 0:
@@ -263,7 +264,7 @@
     lax.fori_loop(0, members, turn_grid, 0)
     loads[4].wait()
 
-    gb = 32
+    gb = 16
 
     def forward(m, _):
         for one in halo_copies(m):
@@ -274,11 +275,10 @@
 
         linear = dot(hits[...], proj[m]) + count * tgt[m].astype(F32)
         for at in range(0, rows, gb):
-            got = dot(pick[:, at:at + gb, :].reshape(nbrs * gb, ext), proj[m]).astype(BF)
-            got = got.reshape(nbrs, gb, width)
+            got = dot(pick[:, at:at + gb, :].reshape(nbrs * gb, ext), proj[m]).reshape(nbrs, gb, width)
             for c in range(0, width, 256):
                 cols = slice(c, c + 256)
-                base = tgt[m, at:at + gb, cols]
+                base = tgt[m, at:at + gb, cols].astype(F32)
                 acc = None
                 acc_s = None
                 for k in range(nbrs):
@@ -289,10 +289,9 @@
                     s = (t + u) - t * p
                     acc = p if k == 0 else acc + p
                     acc_s = s if k == 0 else acc_s + s
-                    slope[m, k, at:at + gb, cols] = s
-                total = linear[at:at + gb, cols] + acc.astype(F32)
-                agg[m, at:at + gb, cols] = (0.25 * total).astype(BF)
-                slope_sum[m, at:at + gb, cols] = (acc_s.astype(F32) + count[at:at + gb]).astype(BF)
+                    slope[m, k, at:at + gb, cols] = s.astype(BF)
+                agg[m, at:at + gb, cols] = (0.25 * (linear[at:at + gb, cols] + acc)).astype(BF)
+                slope_sum[m, at:at + gb, cols] = (acc_s + count[at:at + gb]).astype(BF)
 
         h = grid[m].astype(F32) + dot(agg[m], wmix[...])
         mean = jnp.sum(h, axis=1, keepdims=True) * (1.0 / width)
@@ -515,8 +514,6 @@
         scratch_shapes=[
             pltpu.VMEM((members, rows, width), BF),
             pltpu.VMEM((members, rows, width), BF),
-            pltpu.VMEM((members, rows, width), BF),
-            pltpu.VMEM((members, rows, width), BF),
             pltpu.VMEM((width, width), BF),
             pltpu.VMEM((width, width), BF),
             pltpu.VMEM((width, width), BF),
@@ -527,7 +524,7 @@
             pltpu.VMEM((ext, nbrs * rows), BF),
             pltpu.VMEM((rows, ext), BF),
             pltpu.VMEM((ext, rows), BF),
-            pltpu.VMEM((nbrs, rows, 128), BF),
+            pltpu.VMEM((nbrs, rows, 128), F32),
             pltpu.VMEM((members, ext, width), BF),
             pltpu.VMEM((members, rows, width), BF),
             pltpu.VMEM((members, nbrs, rows, width), BF),

time: 85.4 us -> 89.3 us (1.046)
  Pallas kernels: 84.4 us -> 88.4 us
    pallas_call x1, Pallas kernels: 81.5 us -> 85.4 us  [on_device(): pl.pallas_call(body_, out_shape=[sds((members, rows, width), BF), sds((me...]
where the time goes in v8:
time: 89.3 us; the launch traced here: 89.2 us
  Pallas kernels  88.4 us (99%)
    pallas_call x1, Pallas kernels, on_device(): pl.pallas_call(body_, out_shape=[sds((members, rows, width), BF), sds((me...  85.4 us
    pallas_call x1, Pallas kernels, hand_over(): pl.pallas_call(move, out_shape=[jax.ShapeDtypeStruct(a.shape, a.dtype) fo...  2.99 us

profile of v8, /device:TPU:0, one launch (start us, length us, event | category | flops | bytes accessed | tf_op | source)
XLA Modules:
  0.0 89.2 jit_solution(44729364670417042)
XLA Ops:
  0.6 85.4 %shard_map.145 = (bf16[4,128,1024]{2,1,0:T(8,128)(2,1)}, bf16[4,128,1024]{2,1,0:T(8,128)(2,1)}, f32[16,1024]{1,0:T(8,128)}, f32[16,1024]{1,0:T(8,128)}, f32[16,1024]{1,0:T(8,128)}, /*index=5*/f32[16,100]{1,0:T(8,128)}) custom-call(bf16[4,128,1024]{2,1,0:T(8,128)(2,1)} %refs_0_.1, bf16[4,128,1024]{2,1,0:T(8,128)(2,1)} %refs_1_.1, bf16[1024,1024]{1,0:T(8,128)(2,1)} %refs_2_.1, ...), custom_call_target="tpu_custom_call" | custom-call | flops 40000000000 | bytes 30000000 | tf_op jit(solution)/shard_map/pallas_call | solution.py:502
  86.0 3.0 %shard_map.146 = (bf16[4,128,1024]{2,1,0:T(8,128)(2,1)}, bf16[4,128,1024]{2,1,0:T(8,128)(2,1)}, f32[16,1024]{1,0:T(8,128)}, f32[16,1024]{1,0:T(8,128)}, f32[16,1024]{1,0:T(8,128)}, /*index=5*/f32[16,100]{1,0:T(8,128)}) custom-call(bf16[4,128,1024]{2,1,0:T(8,128)(2,1)} %get-tuple-element.12.refs_0_, bf16[4,128,1024]{2,1,0:T(8,128)(2,1)} %get-tuple-element.13.refs_1_, ...), custom_call_target="tpu_custom_call" | custom-call | tf_op jit(solution)/shard_map/pallas_call | solution.py:471

commit v9 on v6

--- a/solution.py
+++ b/solution.py
@@ -153,9 +153,9 @@
 
 def body(scale, lat_in, grid_in, wsrc_in, wtgt_in, wmix_in, wout_in, truth_in, area_in, nbr, mask,
          d_latent_out, d_grid_out, o_src, o_tgt, o_mix, o_out,
-         lat, grid, d_latent, d_grid, wsrc, wtgt, wmix, wout, truth, area,
-         pick, pick_t, hits, hits_t, maskb, proj, tgt, slope, slope_sum, agg, normed, inv, ys, dys, dh, dq, dpe,
-         agg_x, normed_x, grid_x, lat_x,
+         lat, grid, wsrc, wtgt, wmix, wout, truth, area,
+         pick, pick_t, hits_t, maskb, proj, tgt, slope, slope_sum, agg, normed, inv, ys, dys, dh, dq, dpe,
+         agg_x, grid_x, lat_x,
          halo, rims, *rest):
     send_sem, recv_sem, halo_send, halo_recv, rim_send, rim_recv, y_send, y_recv, load_sem = rest[-9:]
     bufs = rest[:-9]
@@ -165,6 +165,7 @@
     ext = rows + 2 * HALO
     tiles = width // CW
     flat = members * rows
+    d_latent, d_grid = agg, normed
     place = Place()
     wire = Wire(send_sem, recv_sem)
 
@@ -193,7 +194,7 @@
         return copies(lat, 0, rows - HALO, halo, (halo_send, halo_recv), (m,), slice(None))
 
     def rim_copies(m, c):
-        return copies(dpe, 0, HALO + rows, rims, (rim_send, rim_recv), (m, c), pl.ds(c * CW, CW))
+        return copies(dpe, rows, rows + HALO, rims, (rim_send, rim_recv), (m, c), pl.ds(c * CW, CW))
 
     def y_copy(m):
         return pltpu.make_async_remote_copy(
@@ -214,7 +215,8 @@
     wout[...] = jnp.zeros_like(wout)
     wout[0:fields, :] = wout_in[...]
 
-    code = jnp.where(mask[...] != 0, nbr[...], -1).astype(F32)
+    near = jnp.where(nbr[...] < HALO, nbr[...] + rows, jnp.where(nbr[...] < HALO + rows, nbr[...] - HALO, nbr[...]))
+    code = jnp.where(mask[...] != 0, near, -1).astype(F32)
     code_t = jnp.concatenate([code, jnp.zeros((rows - nbrs, rows), F32)], axis=0).T
     lane = lax.broadcasted_iota(jnp.int32, (rows, ext), 1).astype(F32)
     sub = lax.broadcasted_iota(jnp.int32, (ext, rows), 0).astype(F32)
@@ -229,10 +231,10 @@
         count = count + on
         pick_t[:, k * rows:(k + 1) * rows] = one_t
         if k == 0:
-            hits[...] = one
+            pick[nbrs] = one
             hits_t[...] = one_t
         else:
-            hits[...] += one
+            pick[nbrs] += one
             hits_t[...] += one_t
 
     def columns(step, first=0, last=tiles):
@@ -248,7 +250,7 @@
 
     def own_src(cols):
         got = (0.5 * dot(lat[...].reshape(flat, width), wsrc[:, cols]).astype(BF)).astype(BF)
-        proj[:, HALO:HALO + rows, cols] = got.reshape(members, rows, CW)
+        proj[:, 0:rows, cols] = got.reshape(members, rows, CW)
 
     loads[1].wait()
     loads[2].wait()
@@ -258,6 +260,7 @@
 
     def turn_grid(m, _):
         grid_x[:, pl.ds(pl.multiple_of(m * rows, rows), rows)] = grid[m].T
+        lat_x[:, pl.ds(pl.multiple_of(m * ext, ext), rows)] = lat[m].T
         return 0
 
     lax.fori_loop(0, members, turn_grid, 0)
@@ -265,17 +268,11 @@
 
     gb = 32
 
-    def forward(m, _):
-        for one in halo_copies(m):
-            one.wait()
-        edge = (0.5 * dot(halo[m], wsrc[...]).astype(BF)).astype(BF)
-        proj[m, 0:HALO] = edge[0:HALO]
-        proj[m, HALO + rows:ext] = edge[HALO:2 * HALO]
-
-        linear = dot(hits[...], proj[m]) + count * tgt[m].astype(F32)
+    def gather(m, _):
         for at in range(0, rows, gb):
-            got = dot(pick[:, at:at + gb, :].reshape(nbrs * gb, ext), proj[m]).astype(BF)
-            got = got.reshape(nbrs, gb, width)
+            both = dot(pick[:, at:at + gb, :].reshape((nbrs + 1) * gb, ext), proj[m])
+            got = both[0:nbrs * gb].astype(BF).reshape(nbrs, gb, width)
+            linear = both[nbrs * gb:] + count[at:at + gb] * tgt[m, at:at + gb, :].astype(F32)
             for c in range(0, width, 256):
                 cols = slice(c, c + 256)
                 base = tgt[m, at:at + gb, cols]
@@ -290,29 +287,39 @@
                     acc = p if k == 0 else acc + p
                     acc_s = s if k == 0 else acc_s + s
                     slope[m, k, at:at + gb, cols] = s
-                total = linear[at:at + gb, cols] + acc.astype(F32)
+                total = linear[:, cols] + acc.astype(F32)
                 agg[m, at:at + gb, cols] = (0.25 * total).astype(BF)
                 slope_sum[m, at:at + gb, cols] = (acc_s.astype(F32) + count[at:at + gb]).astype(BF)
 
-        h = grid[m].astype(F32) + dot(agg[m], wmix[...])
+        return 0
+
+    def forward(i, _):
+        two = pl.ds(2 * i, 2)
+        for j in range(2):
+            for one in halo_copies(2 * i + j):
+                one.wait()
+        edge = (0.5 * dot(halo[two].reshape(2 * rows, width), wsrc[...]).astype(BF)).astype(BF)
+        proj[two, rows:ext] = edge.reshape(2, rows, width)
+        lax.fori_loop(2 * i, 2 * i + 2, gather, 0)
+        h = dot(agg[two].reshape(2 * rows, width), wmix[...]) + grid[two].reshape(2 * rows, width).astype(F32)
         mean = jnp.sum(h, axis=1, keepdims=True) * (1.0 / width)
         centre = h - mean
         var = jnp.sum(centre * centre, axis=1, keepdims=True) * (1.0 / width)
         r = lax.rsqrt(var + EPS)
-        inv[m] = jnp.broadcast_to(r, (rows, 128))
-        normed[m] = (centre * r).astype(BF)
-        ys[m] = dot_nt(normed[m], wout[...])
-        y_copy(m).start()
-        return 0
-
-    lax.fori_loop(0, members, forward, 0)
+        inv[two] = jnp.broadcast_to(r, (2 * rows, 128)).reshape(2, rows, 128)
+        unit = (centre * r).astype(BF)
+        normed[two] = unit.reshape(2, rows, width)
+        ys[two] = dot_nt(unit, wout[...]).reshape(2, rows, FP)
+        for j in range(2):
+            y_copy(2 * i + j).start()
+        return 0
+
+    lax.fori_loop(0, members // 2, forward, 0)
 
     def turn(m, _):
         at = pl.ds(pl.multiple_of(m * rows, rows), rows)
         agg_x[:, at] = agg[m].T
-        normed_x[:, at] = normed[m].T
-        around = jnp.concatenate([halo[m, 0:HALO], lat[m], halo[m, HALO:2 * HALO]], axis=0)
-        lat_x[:, pl.ds(pl.multiple_of(m * ext, ext), ext)] = around.T
+        lat_x[:, pl.ds(pl.multiple_of(m * ext + rows, rows), rows)] = halo[m].T
         return 0
 
     lax.fori_loop(0, members, turn, 0)
@@ -360,7 +367,8 @@
     put(mix[0].part, mix_grad(pl.ds(0, CW)))
     mix[0].start()
     put(mix[1].part, mix_grad(pl.ds(CW, CW)))
-    put(mix[1].part, product(normed_x, dys[...]), CW)
+    turned = jnp.concatenate([dys[m].T for m in range(members)], axis=1)
+    put(mix[1].part, dot(turned, normed[...].reshape(flat, width)).T.astype(BF), CW)
     mix[1].start()
 
     def mix_back(cols):
@@ -433,7 +441,7 @@
         for c in range(tiles):
             for one in rim_copies(m, c):
                 one.wait()
-        dq[m] = (dpe[m, HALO:HALO + rows].astype(F32) + rims[m].astype(F32)).astype(BF)
+        dq[m] = (dpe[m, 0:rows].astype(F32) + rims[m].astype(F32)).astype(BF)
         return 0
 
     lax.fori_loop(0, members, sum_rims, 0)
@@ -459,22 +467,23 @@
 
 def hand_over(arrays):
     count = len(arrays)
+    steps = arrays[0].shape[0]
 
     def move(*refs):
-        sems = refs[-1]
-        moves = [pltpu.make_async_copy(refs[i], refs[count + i], sems.at[i]) for i in range(count)]
-        for one in moves:
-            one.start()
-        for one in moves:
-            one.wait()
-
-    anywhere = pl.BlockSpec(memory_space=pl.ANY)
+        for i in range(count):
+            refs[count + i][...] = refs[i][...]
+
+    def spec(a):
+        if a.ndim == 3:
+            return pl.BlockSpec((1, *a.shape[1:]), lambda i: (i, 0, 0))
+        return pl.BlockSpec(a.shape, lambda i: (0, 0))
+
     return pl.pallas_call(
         move,
+        grid=(steps,),
         out_shape=[jax.ShapeDtypeStruct(a.shape, a.dtype) for a in arrays],
-        in_specs=[pl.BlockSpec(memory_space=pltpu.VMEM)] * count,
-        out_specs=[anywhere] * count,
-        scratch_shapes=[pltpu.SemaphoreType.DMA((count,))],
+        in_specs=[spec(a) for a in arrays],
+        out_specs=[spec(a) for a in arrays],
     )(*arrays)
 
 
@@ -515,17 +524,14 @@
         scratch_shapes=[
             pltpu.VMEM((members, rows, width), BF),
             pltpu.VMEM((members, rows, width), BF),
-            pltpu.VMEM((members, rows, width), BF),
-            pltpu.VMEM((members, rows, width), BF),
             pltpu.VMEM((width, width), BF),
             pltpu.VMEM((width, width), BF),
             pltpu.VMEM((width, width), BF),
             pltpu.VMEM((FP, width), BF),
             pltpu.VMEM((FP, rows), F32),
             pltpu.VMEM((rows, FP), F32),
-            pltpu.VMEM((nbrs, rows, ext), BF),
+            pltpu.VMEM((nbrs + 1, rows, ext), BF),
             pltpu.VMEM((ext, nbrs * rows), BF),
-            pltpu.VMEM((rows, ext), BF),
             pltpu.VMEM((ext, rows), BF),
             pltpu.VMEM((nbrs, rows, 128), BF),
             pltpu.VMEM((members, ext, width), BF),
@@ -540,7 +546,6 @@
             pltpu.VMEM((members, rows, width), BF),
             pltpu.VMEM((members, rows, width), BF),
             pltpu.VMEM((members, ext, width), BF),
-            pltpu.VMEM((width, members * rows), BF),
             pltpu.VMEM((width, members * rows), BF),
             pltpu.VMEM((width, members * rows), BF),
             pltpu.VMEM((width, members * ext), BF),

time: 85.4 us -> 88 us (1.030)
  Pallas kernels: 84.4 us -> 87 us
    pallas_call x1, Pallas kernels: 81.5 us -> 83.1 us  [on_device(): pl.pallas_call(body_, out_shape=[sds((members, rows, width), BF), sds((me...]
where the time goes in v9:
time: 88 us; the launch traced here: 87.8 us
  Pallas kernels  87 us (99%)
    pallas_call x1, Pallas kernels, on_device(): pl.pallas_call(body_, out_shape=[sds((members, rows, width), BF), sds((me...  83.1 us
    pallas_call x1, Pallas kernels, hand_over(): pl.pallas_call(move, grid=(steps,), out_shape=[jax.ShapeDtypeStruct(a.sha...  3.85 us

profile of v9, /device:TPU:0, one launch (start us, length us, event | category | flops | bytes accessed | tf_op | source)
XLA Modules:
  0.0 87.8 jit_solution(3050671624678371596)
XLA Ops:
  0.6 83.1 %shard_map.145 = (bf16[4,128,1024]{2,1,0:T(8,128)(2,1)}, bf16[4,128,1024]{2,1,0:T(8,128)(2,1)}, f32[16,1024]{1,0:T(8,128)}, f32[16,1024]{1,0:T(8,128)}, f32[16,1024]{1,0:T(8,128)}, /*index=5*/f32[16,100]{1,0:T(8,128)}) custom-call(bf16[4,128,1024]{2,1,0:T(8,128)(2,1)} %refs_0_.1, bf16[4,128,1024]{2,1,0:T(8,128)(2,1)} %refs_1_.1, bf16[1024,1024]{1,0:T(8,128)(2,1)} %refs_2_.1, ...), custom_call_target="tpu_custom_call" | custom-call | flops 40000000000 | bytes 30000000 | tf_op jit(solution)/shard_map/pallas_call | solution.py:512
  83.8 3.9 %shard_map.146 = (bf16[4,128,1024]{2,1,0:T(8,128)(2,1)}, bf16[4,128,1024]{2,1,0:T(8,128)(2,1)}, f32[16,1024]{1,0:T(8,128)}, f32[16,1024]{1,0:T(8,128)}, f32[16,1024]{1,0:T(8,128)}, /*index=5*/f32[16,100]{1,0:T(8,128)}) custom-call(bf16[4,128,1024]{2,1,0:T(8,128)(2,1)} %get-tuple-element.12.refs_0_, bf16[4,128,1024]{2,1,0:T(8,128)(2,1)} %get-tuple-element.13.refs_1_, ...), custom_call_target="tpu_custom_call" | custom-call | tf_op jit(solution)/shard_map/pallas_call | solution.py:481

commit v10 on v6

--- a/solution.py
+++ b/solution.py
@@ -153,9 +153,9 @@
 
 def body(scale, lat_in, grid_in, wsrc_in, wtgt_in, wmix_in, wout_in, truth_in, area_in, nbr, mask,
          d_latent_out, d_grid_out, o_src, o_tgt, o_mix, o_out,
-         lat, grid, d_latent, d_grid, wsrc, wtgt, wmix, wout, truth, area,
+         lat, grid, wsrc, wtgt, wmix, wout, truth, area,
          pick, pick_t, hits, hits_t, maskb, proj, tgt, slope, slope_sum, agg, normed, inv, ys, dys, dh, dq, dpe,
-         agg_x, normed_x, grid_x, lat_x,
+         agg_x, grid_x, lat_x,
          halo, rims, *rest):
     send_sem, recv_sem, halo_send, halo_recv, rim_send, rim_recv, y_send, y_recv, load_sem = rest[-9:]
     bufs = rest[:-9]
@@ -165,6 +165,7 @@
     ext = rows + 2 * HALO
     tiles = width // CW
     flat = members * rows
+    d_latent, d_grid = agg, normed
     place = Place()
     wire = Wire(send_sem, recv_sem)
 
@@ -193,7 +194,7 @@
         return copies(lat, 0, rows - HALO, halo, (halo_send, halo_recv), (m,), slice(None))
 
     def rim_copies(m, c):
-        return copies(dpe, 0, HALO + rows, rims, (rim_send, rim_recv), (m, c), pl.ds(c * CW, CW))
+        return copies(dpe, rows, rows + HALO, rims, (rim_send, rim_recv), (m, c), pl.ds(c * CW, CW))
 
     def y_copy(m):
         return pltpu.make_async_remote_copy(
@@ -203,9 +204,12 @@
 
     loads[0].wait()
     pl.semaphore_wait(barrier, len(place.partners))
-    for m in range(members):
+
+    def send_halo(m):
         for one in halo_copies(m):
             one.start()
+
+    send_halo(0)
 
     truth[...] = jnp.zeros_like(truth)
     truth[0:fields, :] = truth_in[...]
@@ -214,7 +218,8 @@
     wout[...] = jnp.zeros_like(wout)
     wout[0:fields, :] = wout_in[...]
 
-    code = jnp.where(mask[...] != 0, nbr[...], -1).astype(F32)
+    near = jnp.where(nbr[...] < HALO, nbr[...] + rows, jnp.where(nbr[...] < HALO + rows, nbr[...] - HALO, nbr[...]))
+    code = jnp.where(mask[...] != 0, near, -1).astype(F32)
     code_t = jnp.concatenate([code, jnp.zeros((rows - nbrs, rows), F32)], axis=0).T
     lane = lax.broadcasted_iota(jnp.int32, (rows, ext), 1).astype(F32)
     sub = lax.broadcasted_iota(jnp.int32, (ext, rows), 0).astype(F32)
@@ -248,16 +253,20 @@
 
     def own_src(cols):
         got = (0.5 * dot(lat[...].reshape(flat, width), wsrc[:, cols]).astype(BF)).astype(BF)
-        proj[:, HALO:HALO + rows, cols] = got.reshape(members, rows, CW)
-
+        proj[:, 0:rows, cols] = got.reshape(members, rows, CW)
+
+    send_halo(1)
     loads[1].wait()
     loads[2].wait()
     columns(own_tgt)
+    send_halo(2)
     loads[3].wait()
     columns(own_src)
+    send_halo(3)
 
     def turn_grid(m, _):
         grid_x[:, pl.ds(pl.multiple_of(m * rows, rows), rows)] = grid[m].T
+        lat_x[:, pl.ds(pl.multiple_of(m * ext, ext), rows)] = lat[m].T
         return 0
 
     lax.fori_loop(0, members, turn_grid, 0)
@@ -269,8 +278,7 @@
         for one in halo_copies(m):
             one.wait()
         edge = (0.5 * dot(halo[m], wsrc[...]).astype(BF)).astype(BF)
-        proj[m, 0:HALO] = edge[0:HALO]
-        proj[m, HALO + rows:ext] = edge[HALO:2 * HALO]
+        proj[m, rows:ext] = edge
 
         linear = dot(hits[...], proj[m]) + count * tgt[m].astype(F32)
         for at in range(0, rows, gb):
@@ -310,9 +318,7 @@
     def turn(m, _):
         at = pl.ds(pl.multiple_of(m * rows, rows), rows)
         agg_x[:, at] = agg[m].T
-        normed_x[:, at] = normed[m].T
-        around = jnp.concatenate([halo[m, 0:HALO], lat[m], halo[m, HALO:2 * HALO]], axis=0)
-        lat_x[:, pl.ds(pl.multiple_of(m * ext, ext), ext)] = around.T
+        lat_x[:, pl.ds(pl.multiple_of(m * ext + rows, rows), rows)] = halo[m].T
         return 0
 
     lax.fori_loop(0, members, turn, 0)
@@ -360,7 +366,8 @@
     put(mix[0].part, mix_grad(pl.ds(0, CW)))
     mix[0].start()
     put(mix[1].part, mix_grad(pl.ds(CW, CW)))
-    put(mix[1].part, product(normed_x, dys[...]), CW)
+    turned = jnp.concatenate([dys[m].T for m in range(members)], axis=1)
+    put(mix[1].part, dot(turned, normed[...].reshape(flat, width)).T.astype(BF), CW)
     mix[1].start()
 
     def mix_back(cols):
@@ -433,7 +440,7 @@
         for c in range(tiles):
             for one in rim_copies(m, c):
                 one.wait()
-        dq[m] = (dpe[m, HALO:HALO + rows].astype(F32) + rims[m].astype(F32)).astype(BF)
+        dq[m] = (dpe[m, 0:rows].astype(F32) + rims[m].astype(F32)).astype(BF)
         return 0
 
     lax.fori_loop(0, members, sum_rims, 0)
@@ -515,8 +522,6 @@
         scratch_shapes=[
             pltpu.VMEM((members, rows, width), BF),
             pltpu.VMEM((members, rows, width), BF),
-            pltpu.VMEM((members, rows, width), BF),
-            pltpu.VMEM((members, rows, width), BF),
             pltpu.VMEM((width, width), BF),
             pltpu.VMEM((width, width), BF),
             pltpu.VMEM((width, width), BF),
@@ -540,7 +545,6 @@
             pltpu.VMEM((members, rows, width), BF),
             pltpu.VMEM((members, rows, width), BF),
             pltpu.VMEM((members, ext, width), BF),
-            pltpu.VMEM((width, members * rows), BF),
             pltpu.VMEM((width, members * rows), BF),
             pltpu.VMEM((width, members * rows), BF),
             pltpu.VMEM((width, members * ext), BF),

time: 85.4 us -> 84.7 us (level)
  no operation moved by 1% of the time
where the time goes in v10:
time: 84.7 us; the launch traced here: 84.5 us
  Pallas kernels  83.7 us (99%)
    pallas_call x1, Pallas kernels, on_device(): pl.pallas_call(body_, out_shape=[sds((members, rows, width), BF), sds((me...  80.8 us
    pallas_call x1, Pallas kernels, hand_over(): pl.pallas_call(move, out_shape=[jax.ShapeDtypeStruct(a.shape, a.dtype) fo...  2.99 us

profile of v10, /device:TPU:0, one launch (start us, length us, event | category | flops | bytes accessed | tf_op | source)
XLA Modules:
  0.0 84.5 jit_solution(969562028206787152)
XLA Ops:
  0.6 80.8 %shard_map.145 = (bf16[4,128,1024]{2,1,0:T(8,128)(2,1)}, bf16[4,128,1024]{2,1,0:T(8,128)(2,1)}, f32[16,1024]{1,0:T(8,128)}, f32[16,1024]{1,0:T(8,128)}, f32[16,1024]{1,0:T(8,128)}, /*index=5*/f32[16,100]{1,0:T(8,128)}) custom-call(bf16[4,128,1024]{2,1,0:T(8,128)(2,1)} %refs_0_.1, bf16[4,128,1024]{2,1,0:T(8,128)(2,1)} %refs_1_.1, bf16[1024,1024]{1,0:T(8,128)(2,1)} %refs_2_.1, ...), custom_call_target="tpu_custom_call" | custom-call | flops 40000000000 | bytes 30000000 | tf_op jit(solution)/shard_map/pallas_call | solution.py:510
  81.4 3.0 %shard_map.146 = (bf16[4,128,1024]{2,1,0:T(8,128)(2,1)}, bf16[4,128,1024]{2,1,0:T(8,128)(2,1)}, f32[16,1024]{1,0:T(8,128)}, f32[16,1024]{1,0:T(8,128)}, f32[16,1024]{1,0:T(8,128)}, /*index=5*/f32[16,100]{1,0:T(8,128)}) custom-call(bf16[4,128,1024]{2,1,0:T(8,128)(2,1)} %get-tuple-element.12.refs_0_, bf16[4,128,1024]{2,1,0:T(8,128)(2,1)} %get-tuple-element.13.refs_1_, ...), custom_call_target="tpu_custom_call" | custom-call | tf_op jit(solution)/shard_map/pallas_call | solution.py:479

commit v11 on v10

--- a/solution.py
+++ b/solution.py
@@ -19,7 +19,7 @@
 FP = 128
 MIX_CUTS = ((0, 512), (512, 512 + FP))
 TGT_CUTS = ((0, 512), (512, 512))
-SRC_CUTS = ((0, 256), (256, 256), (512, 256), (768, 256))
+SRC_CUTS = ((0, 512), (512, 512))
 
 
 def dot(a, b):
@@ -193,8 +193,8 @@
     def halo_copies(m):
         return copies(lat, 0, rows - HALO, halo, (halo_send, halo_recv), (m,), slice(None))
 
-    def rim_copies(m, c):
-        return copies(dpe, rows, rows + HALO, rims, (rim_send, rim_recv), (m, c), pl.ds(c * CW, CW))
+    def rim_copies(m):
+        return copies(dpe, rows, rows + HALO, rims, (rim_send, rim_recv), (m,), slice(None))
 
     def y_copy(m):
         return pltpu.make_async_remote_copy(
@@ -387,48 +387,42 @@
     tgt_sum[1].start()
     each(mix, "s1")
 
-    def spread(c, first, last):
-        cols = pl.ds(c * CW, CW)
-
-        def member(m, _):
+    def spread(m):
+        def column(cols):
             d = tgt[m, :, cols]
             for k in range(nbrs):
                 slope[m, k, :, cols] = slope[m, k, :, cols] * d
             edges = slope[m, :, :, cols].reshape(nbrs * rows, CW)
             dpe[m, :, cols] = (dot(pick_t[...], edges) + dot(hits_t[...], d)).astype(BF)
-            for one in rim_copies(m, c):
-                one.start()
-            return 0
-
-        lax.fori_loop(first, last, member, 0)
+
+        columns(column)
+        for one in rim_copies(m):
+            one.start()
 
     def src_grad(c):
-        block = product(lat_x, dpe[:, :, c * CW:(c + 1) * CW])
-        for i in range(2):
-            put(src[2 * c + i].part, block[:, i * 256:(i + 1) * 256])
+        put(src[c].part, product(lat_x, dpe[:, :, c * CW:(c + 1) * CW]))
 
     def grid_back(cols):
         got = dot_nt(dq[...].reshape(flat, width), wtgt[cols, :]).reshape(members, rows, CW)
         d_grid[:, :, cols] = (dh[:, :, cols].astype(F32) + got).astype(BF)
 
-    spread(0, 0, 2)
+    spread(0)
     each(tgt_sum, "s1")
-    spread(0, 2, 4)
+    spread(1)
+    spread(2)
     each(mix, "s2")
+    spread(3)
     src_grad(0)
-    each(src[:2], "start")
-    spread(1, 0, 2)
+    src[0].start()
     each(tgt_sum, "s2")
-    each(src[:2], "s1")
-    spread(1, 2, 4)
+    src_grad(1)
+    src[1].start()
     each(mix, "s3")
-    src_grad(1)
-    each(src[2:], "start")
+    src[0].s1()
+    columns(grid_back, 0, 1)
+    src[1].s1()
+    columns(grid_back, 1, 2)
     each(tgt_sum, "s3")
-    columns(grid_back, 0, 1)
-    each(src[2:], "s1")
-    each(src[:2], "s2")
-    columns(grid_back, 1, 2)
     out_grid = pltpu.make_async_copy(d_grid, d_grid_out, load_sem.at[5])
     out_grid.start()
     o_mix[:, 0:512] = mix[0].s4(scale)
@@ -437,9 +431,8 @@
     o_out[...] = last[:, width - 512:width - 512 + fields]
 
     def sum_rims(m, _):
-        for c in range(tiles):
-            for one in rim_copies(m, c):
-                one.wait()
+        for one in rim_copies(m):
+            one.wait()
         dq[m] = (dpe[m, 0:rows].astype(F32) + rims[m].astype(F32)).astype(BF)
         return 0
 
@@ -450,14 +443,14 @@
         d_latent[:, :, cols] = got.astype(BF)
 
     columns(latent_back, 0, 1)
-    each(src[:2], "s3")
+    src[0].s2()
     columns(latent_back, 1, 2)
     out_latent = pltpu.make_async_copy(d_latent, d_latent_out, load_sem.at[6])
     out_latent.start()
-    each(src[2:], "s2")
+    src[1].s2()
     for one, (first, size) in zip(tgt_sum, TGT_CUTS):
         o_tgt[:, first:first + size] = one.s4(scale)
-    each(src[2:], "s3")
+    each(src, "s3")
     out_grid.wait()
     out_latent.wait()
     for one, (first, size) in zip(src, SRC_CUTS):
@@ -466,22 +459,34 @@
 
 def hand_over(arrays):
     count = len(arrays)
+    pieces = [(i, m) for i, a in enumerate(arrays) for m in range(a.shape[0] if a.ndim == 3 else 1)]
 
     def move(*refs):
-        sems = refs[-1]
-        moves = [pltpu.make_async_copy(refs[i], refs[count + i], sems.at[i]) for i in range(count)]
-        for one in moves:
+        held, (came, went) = refs[2 * count:3 * count], refs[3 * count:]
+
+        def at(ref, i, m):
+            return ref.at[m] if arrays[i].ndim == 3 else ref
+
+        ins = [pltpu.make_async_copy(at(refs[i], i, m), at(held[i], i, m), came.at[n])
+               for n, (i, m) in enumerate(pieces)]
+        outs = [pltpu.make_async_copy(at(held[i], i, m), at(refs[count + i], i, m), went.at[n])
+                for n, (i, m) in enumerate(pieces)]
+        for one in ins:
             one.start()
-        for one in moves:
+        for one, other in zip(ins, outs):
+            one.wait()
+            other.start()
+        for one in outs:
             one.wait()
 
     anywhere = pl.BlockSpec(memory_space=pl.ANY)
     return pl.pallas_call(
         move,
         out_shape=[jax.ShapeDtypeStruct(a.shape, a.dtype) for a in arrays],
-        in_specs=[pl.BlockSpec(memory_space=pltpu.VMEM)] * count,
+        in_specs=[anywhere] * count,
         out_specs=[anywhere] * count,
-        scratch_shapes=[pltpu.SemaphoreType.DMA((count,))],
+        scratch_shapes=[*[pltpu.VMEM(a.shape, a.dtype) for a in arrays],
+                        pltpu.SemaphoreType.DMA((len(pieces),)), pltpu.SemaphoreType.DMA((len(pieces),))],
     )(*arrays)
 
 
@@ -555,8 +560,8 @@
             pltpu.SemaphoreType.DMA((ncopies,)),
             pltpu.SemaphoreType.DMA((2, members)),
             pltpu.SemaphoreType.DMA((2, members)),
-            pltpu.SemaphoreType.DMA((2, members, width // CW)),
-            pltpu.SemaphoreType.DMA((2, members, width // CW)),
+            pltpu.SemaphoreType.DMA((2, members)),
+            pltpu.SemaphoreType.DMA((2, members)),
             pltpu.SemaphoreType.DMA((members,)),
             pltpu.SemaphoreType.DMA((members,)),
             pltpu.SemaphoreType.DMA((8,)),

time: 84.7 us -> 83 us (0.980); the launches traced: 84.5 us -> 81.8 us
  Pallas kernels: 83.7 us -> 81 us
    pallas_call x1, Pallas kernels: 80.8 us -> 78.5 us  [on_device(): pl.pallas_call(body_, out_shape=[sds((members, rows, width), BF), sds((me...]
where the time goes in v11:
time: 83 us; the launch traced here: 81.8 us
  Pallas kernels  81 us (98%)
    pallas_call x1, Pallas kernels, on_device(): pl.pallas_call(body_, out_shape=[sds((members, rows, width), BF), sds((me...  78.5 us
    pallas_call x1, Pallas kernels, hand_over(): pl.pallas_call(move, out_shape=[jax.ShapeDtypeStruct(a.shape, a.dtype) fo...  2.53 us

profile of v11, /device:TPU:0, one launch (start us, length us, event | category | flops | bytes accessed | tf_op | source)
XLA Modules:
  0.0 81.8 jit_solution(9384195581053155222)
XLA Ops:
  0.6 78.5 %shard_map.145 = (bf16[4,128,1024]{2,1,0:T(8,128)(2,1)}, bf16[4,128,1024]{2,1,0:T(8,128)(2,1)}, f32[16,1024]{1,0:T(8,128)}, f32[16,1024]{1,0:T(8,128)}, f32[16,1024]{1,0:T(8,128)}, /*index=5*/f32[16,100]{1,0:T(8,128)}) custom-call(bf16[4,128,1024]{2,1,0:T(8,128)(2,1)} %refs_0_.1, bf16[4,128,1024]{2,1,0:T(8,128)(2,1)} %refs_1_.1, bf16[1024,1024]{1,0:T(8,128)(2,1)} %refs_2_.1, ...), custom_call_target="tpu_custom_call" | custom-call | flops 40000000000 | bytes 30000000 | tf_op jit(solution)/shard_map/pallas_call | solution.py:515
  79.1 2.5 %shard_map.146 = (bf16[4,128,1024]{2,1,0:T(8,128)(2,1)}, bf16[4,128,1024]{2,1,0:T(8,128)(2,1)}, f32[16,1024]{1,0:T(8,128)}, f32[16,1024]{1,0:T(8,128)}, f32[16,1024]{1,0:T(8,128)}, /*index=5*/f32[16,100]{1,0:T(8,128)}) custom-call(bf16[4,128,1024]{2,1,0:T(8,128)(2,1)} %get-tuple-element.12.refs_0_, bf16[4,128,1024]{2,1,0:T(8,128)(2,1)} %get-tuple-element.13.refs_1_, ...), custom_call_target="tpu_custom_call" | custom-call | tf_op jit(solution)/shard_map/pallas_call | solution.py:483

commit v12 on v11

--- a/solution.py
+++ b/solution.py
@@ -409,15 +409,15 @@
     spread(0)
     each(tgt_sum, "s1")
     spread(1)
+    each(mix, "s2")
     spread(2)
-    each(mix, "s2")
     spread(3)
+    each(tgt_sum, "s2")
     src_grad(0)
     src[0].start()
-    each(tgt_sum, "s2")
+    each(mix, "s3")
     src_grad(1)
     src[1].start()
-    each(mix, "s3")
     src[0].s1()
     columns(grid_back, 0, 1)
     src[1].s1()

time: 83 us -> 84.6 us (1.019)
  Pallas kernels: 81 us -> 83.3 us
    pallas_call x1, Pallas kernels: 78.5 us -> 80.8 us  [on_device(): pl.pallas_call(body_, out_shape=[sds((members, rows, width), BF), sds((me...]
where the time goes in v12:
time: 84.6 us; the launch traced here: 84.1 us
  Pallas kernels  83.3 us (98%)
    pallas_call x1, Pallas kernels, on_device(): pl.pallas_call(body_, out_shape=[sds((members, rows, width), BF), sds((me...  80.8 us
    pallas_call x1, Pallas kernels, hand_over(): pl.pallas_call(move, out_shape=[jax.ShapeDtypeStruct(a.shape, a.dtype) fo...  2.53 us

profile of v12, /device:TPU:0, one launch (start us, length us, event | category | flops | bytes accessed | tf_op | source)
XLA Modules:
  0.0 84.1 jit_solution(656592192138870686)
XLA Ops:
  0.6 80.8 %shard_map.145 = (bf16[4,128,1024]{2,1,0:T(8,128)(2,1)}, bf16[4,128,1024]{2,1,0:T(8,128)(2,1)}, f32[16,1024]{1,0:T(8,128)}, f32[16,1024]{1,0:T(8,128)}, f32[16,1024]{1,0:T(8,128)}, /*index=5*/f32[16,100]{1,0:T(8,128)}) custom-call(bf16[4,128,1024]{2,1,0:T(8,128)(2,1)} %refs_0_.1, bf16[4,128,1024]{2,1,0:T(8,128)(2,1)} %refs_1_.1, bf16[1024,1024]{1,0:T(8,128)(2,1)} %refs_2_.1, ...), custom_call_target="tpu_custom_call" | custom-call | flops 40000000000 | bytes 30000000 | tf_op jit(solution)/shard_map/pallas_call | solution.py:515
  81.4 2.5 %shard_map.146 = (bf16[4,128,1024]{2,1,0:T(8,128)(2,1)}, bf16[4,128,1024]{2,1,0:T(8,128)(2,1)}, f32[16,1024]{1,0:T(8,128)}, f32[16,1024]{1,0:T(8,128)}, f32[16,1024]{1,0:T(8,128)}, /*index=5*/f32[16,100]{1,0:T(8,128)}) custom-call(bf16[4,128,1024]{2,1,0:T(8,128)(2,1)} %get-tuple-element.12.refs_0_, bf16[4,128,1024]{2,1,0:T(8,128)(2,1)} %get-tuple-element.13.refs_1_, ...), custom_call_target="tpu_custom_call" | custom-call | tf_op jit(solution)/shard_map/pallas_call | solution.py:483
